TPU v7x, 32 devices: a whole 2x2x4 slice. The times are simulated.
32 devices in a mesh: ctx: 8 (over z, x), fsdp: 4 (over y, core).
Axes of the slice: x: 2, y: 2, z: 4, core: 2. Of those that a mesh axis runs over, the one named last changes fastest.
Arguments:
- tokens: bfloat16 [4, 2048, 1024], P('fsdp', 'ctx'), may hold values from -6 to 6
- cotangent: bfloat16 [4, 2048, 1024], P('fsdp', 'ctx'), may hold values from -6 to 6
- block_map: int32 [8, 2], replicated, may hold values from 0 to 15, as said below
- positions: int32 [4, 2048], P('fsdp', 'ctx'), may hold values from 0 to 4094, as said below
- attn_gain: float32 [1024], P('fsdp'), may hold values from 0.1 to 1.9
- query_weight: float32 [1024, 2048], P('fsdp'), may hold values from -0.1875 to 0.1875
- key_weight: float32 [1024, 1024], P('fsdp'), may hold values from -0.1875 to 0.1875
- value_weight: float32 [1024, 1024], P('fsdp'), may hold values from -0.1875 to 0.1875
- query_gain: float32 [128], P('fsdp'), may hold values from 1 to 2
- key_gain: float32 [128], P('fsdp'), may hold values from 1 to 2
- out_weight: float32 [2048, 1024], P('fsdp'), may hold values from -1 to 1
- mlp_gain: float32 [1024], P('fsdp'), may hold values from 0.1 to 1.9
- gate_weight: float32 [1024, 3072], P('fsdp'), may hold values from -0.1875 to 0.1875
- up_weight: float32 [1024, 3072], P('fsdp'), may hold values from -0.1875 to 0.1875
- down_weight: float32 [3072, 1024], P('fsdp'), may hold values from -0.15625 to 0.15625
Outputs:
- layer_output: float32 [4, 2048, 1024], P('fsdp', 'ctx')
- input_grad: float32 [4, 2048, 1024], P('fsdp', 'ctx')
- attn_gain_grad: float32 [1024], P('fsdp')
- query_weight_grad: float32 [1024, 2048], P('fsdp')
- key_weight_grad: float32 [1024, 1024], P('fsdp')
- value_weight_grad: float32 [1024, 1024], P('fsdp')
- query_gain_grad: float32 [128], P('fsdp')
- key_gain_grad: float32 [128], P('fsdp')
- out_weight_grad: float32 [2048, 1024], P('fsdp')
- mlp_gain_grad: float32 [1024], P('fsdp')
- gate_weight_grad: float32 [1024, 3072], P('fsdp')
- up_weight_grad: float32 [1024, 3072], P('fsdp')
- down_weight_grad: float32 [3072, 1024], P('fsdp')
Inputs may be any that keep to these rules, and one draw needn't show every extreme that they name: `block_map`: row c is a pair (p, 15 - p) with p below 8; every block number appears exactly once. `positions`: along each sequence, taken in the order of the causal index, the first position is 0 and each next one exceeds the one before by 1 or 2; in one sequence every step is 2.
All inputs are finite; a program needn't handle non-finite values.
Results may differ from a plain program's by a relative error of at most 0.023.
Values may be sent and summed in bfloat16 or wider, within the bound.
A program may use at most 256 MiB of HBM per device.

v0:
```python
import math

import jax
import jax.numpy as jnp
from jax import lax
from jax.sharding import PartitionSpec as P

D = 1024
HQ = 16
HK = 8
HD = 128
BLK = 128


epsilon = 1e-06
theta_base = 1000000.0
masked_value = -1e30


def rms_scale(values):
    return lax.rsqrt(jnp.mean(values * values, axis=-1, keepdims=True) + epsilon)


def norm_back(upstream, values, scale):
    return scale * upstream - values * (scale * scale * scale) * jnp.mean(
        upstream * values, axis=-1, keepdims=True
    )


def rope_tables(positions, head_dim):
    frequency = jnp.exp(
        jnp.arange(0, head_dim, 2).astype(jnp.float32) * (-math.log(theta_base) / head_dim)
    )
    angles = positions.astype(jnp.float32)[..., None] * frequency
    angles = jnp.concatenate([angles, angles], axis=-1)
    return (jnp.cos(angles), jnp.sin(angles))


def rotate(values, cosine, sine_table):
    half_width = values.shape[-1] // 2
    turned = jnp.concatenate([-values[..., half_width:], values[..., :half_width]], axis=-1)
    return values * cosine + turned * sine_table


def unrotate(grads, cosine, sine_table):
    half_width = grads.shape[-1] // 2
    moved = grads * sine_table
    back_turn = jnp.concatenate([moved[..., half_width:], -moved[..., :half_width]], axis=-1)
    return grads * cosine + back_turn


def score_block(grouped, keys_head, allowed, scale):
    scores = (
        jnp.einsum("qgd,sd->gqs", grouped, keys_head, preferred_element_type=jnp.float32) * scale
    )
    return jnp.where(allowed, scores, masked_value)


def body(
    tokens,
    cotangent,
    block_map,
    positions,
    attn_gain,
    query_weight,
    key_weight,
    value_weight,
    query_gain,
    key_gain,
    out_weight,
    mlp_gain,
    gate_weight,
    up_weight,
    down_weight,
):
    seq_count = tokens.shape[0]
    seq_rows = tokens.shape[1]
    total_rows = seq_count * seq_rows
    groups = HQ // HK
    scale = HD ** (-0.5)
    attn_full, query_full, key_full, mlp_full = (
        lax.all_gather(attn_gain, "fsdp", axis=0, tiled=True),
        lax.all_gather(query_gain, "fsdp", axis=0, tiled=True),
        lax.all_gather(key_gain, "fsdp", axis=0, tiled=True),
        lax.all_gather(mlp_gain, "fsdp", axis=0, tiled=True),
    )
    query_w, key_w, value_w, out_w = (
        lax.all_gather(query_weight.astype(jnp.bfloat16), "fsdp", axis=0, tiled=True),
        lax.all_gather(key_weight.astype(jnp.bfloat16), "fsdp", axis=0, tiled=True),
        lax.all_gather(value_weight.astype(jnp.bfloat16), "fsdp", axis=0, tiled=True),
        lax.all_gather(out_weight.astype(jnp.bfloat16), "fsdp", axis=0, tiled=True),
    )
    flat = tokens.astype(jnp.float32).reshape(total_rows, D)
    scale_one = rms_scale(flat)
    normed = (flat * scale_one * attn_full).astype(jnp.bfloat16)
    query_raw = jnp.dot(normed, query_w, preferred_element_type=jnp.float32).reshape(
        total_rows, HQ, HD
    )
    key_raw = jnp.dot(normed, key_w, preferred_element_type=jnp.float32).reshape(total_rows, HK, HD)
    value_low = jnp.dot(normed, value_w, preferred_element_type=jnp.float32).astype(jnp.bfloat16)
    cosine, sine_table = rope_tables(positions.reshape(total_rows), HD)
    cosine = cosine[:, None, :]
    sine_table = sine_table[:, None, :]
    query_scale = rms_scale(query_raw)
    query_unit = query_raw * query_scale
    query_low = rotate(query_unit * query_full, cosine, sine_table).astype(jnp.bfloat16)
    key_scale = rms_scale(key_raw)
    key_unit = key_raw * key_scale
    key_low = rotate(key_unit * key_full, cosine, sine_table).astype(jnp.bfloat16)
    flat_map = block_map.reshape(-1)
    offsets = jnp.arange(BLK, dtype=jnp.int32)
    key_index = (flat_map[:, None] * BLK + offsets[None, :]).reshape(-1)
    own_blocks = lax.dynamic_slice_in_dim(flat_map, lax.axis_index("ctx") * 2, 2)
    query_index = (own_blocks[:, None] * BLK + offsets[None, :]).reshape(-1)
    allowed = query_index[:, None] >= key_index[None, :]
    query_seq = query_low.reshape(seq_count, seq_rows, HK, groups, HD)
    key_seq = key_low.reshape(seq_count, seq_rows, HK * HD)
    value_seq = value_low.reshape(seq_count, seq_rows, HK * HD)

    def forward_head(inputs):
        grouped, keys_head, values_head = inputs
        scores = score_block(grouped, keys_head, allowed, scale)
        row_max = jnp.max(scores, axis=-1, keepdims=True)
        exp_scores = jnp.exp(scores - row_max)
        row_total = jnp.sum(exp_scores, axis=-1, keepdims=True)
        prob_low = (exp_scores / row_total).astype(jnp.bfloat16)
        mixed = jnp.einsum("gqs,sd->qgd", prob_low, values_head, preferred_element_type=jnp.float32)
        return (mixed, row_max + jnp.log(row_total))

    seq_item = 0
    keys_all = lax.all_gather(key_seq[seq_item], "ctx", axis=0, tiled=True)
    values_all = lax.all_gather(value_seq[seq_item], "ctx", axis=0, tiled=True)
    keys_head = jnp.transpose(keys_all.reshape(-1, HK, HD), (1, 0, 2))
    values_head = jnp.transpose(values_all.reshape(-1, HK, HD), (1, 0, 2))
    grouped_head = jnp.transpose(query_seq[seq_item], (1, 0, 2, 3))
    mixed, lse = lax.map(forward_head, (grouped_head, keys_head, values_head))
    mixed_parts = jnp.transpose(mixed, (1, 0, 2, 3)).reshape(seq_rows, HQ * HD)
    lse_parts = [lse]
    gathered = [(grouped_head, keys_head, values_head)]
    attended = mixed_parts.astype(jnp.bfloat16)
    middle = flat + jnp.dot(attended, out_w, preferred_element_type=jnp.float32)
    gate_w, up_w, down_w = (
        lax.all_gather(gate_weight.astype(jnp.bfloat16), "fsdp", axis=0, tiled=True),
        lax.all_gather(up_weight.astype(jnp.bfloat16), "fsdp", axis=0, tiled=True),
        lax.all_gather(down_weight.astype(jnp.bfloat16), "fsdp", axis=0, tiled=True),
    )
    scale_two = rms_scale(middle)
    normed_two = (middle * scale_two * mlp_full).astype(jnp.bfloat16)
    gate = jnp.dot(normed_two, gate_w, preferred_element_type=jnp.float32)
    upward = jnp.dot(normed_two, up_w, preferred_element_type=jnp.float32)
    sigmoid_gate = jax.nn.sigmoid(gate)
    silu_gate = gate * sigmoid_gate
    hidden = (silu_gate * upward).astype(jnp.bfloat16)
    result = middle + jnp.dot(hidden, down_w, preferred_element_type=jnp.float32)
    query_back, key_back, value_back, out_back = (
        lax.all_gather(query_weight.astype(jnp.bfloat16), "fsdp", axis=0, tiled=True),
        lax.all_gather(key_weight.astype(jnp.bfloat16), "fsdp", axis=0, tiled=True),
        lax.all_gather(value_weight.astype(jnp.bfloat16), "fsdp", axis=0, tiled=True),
        lax.all_gather(out_weight.astype(jnp.bfloat16), "fsdp", axis=0, tiled=True),
    )
    gate_back, up_back, down_back = (
        lax.all_gather(gate_weight.astype(jnp.bfloat16), "fsdp", axis=0, tiled=True),
        lax.all_gather(up_weight.astype(jnp.bfloat16), "fsdp", axis=0, tiled=True),
        lax.all_gather(down_weight.astype(jnp.bfloat16), "fsdp", axis=0, tiled=True),
    )
    grad_out = cotangent.astype(jnp.float32).reshape(total_rows, D)
    grad_branch = grad_out.astype(jnp.bfloat16)
    down_grad = jnp.einsum("nf,nd->fd", hidden, grad_branch, preferred_element_type=jnp.float32)
    grad_hidden = jnp.einsum(
        "nd,fd->nf", grad_branch, down_back, preferred_element_type=jnp.float32
    )
    grad_gate = (grad_hidden * upward * sigmoid_gate * (1.0 + gate * (1.0 - sigmoid_gate))).astype(
        jnp.bfloat16
    )
    grad_up = (grad_hidden * silu_gate).astype(jnp.bfloat16)
    gate_grad = jnp.einsum("nd,nf->df", normed_two, grad_gate, preferred_element_type=jnp.float32)
    up_grad = jnp.einsum("nd,nf->df", normed_two, grad_up, preferred_element_type=jnp.float32)
    grad_normed_two = jnp.einsum(
        "nf,df->nd", grad_gate, gate_back, preferred_element_type=jnp.float32
    ) + jnp.einsum("nf,df->nd", grad_up, up_back, preferred_element_type=jnp.float32)
    mlp_local = jnp.sum(grad_normed_two * middle * scale_two, axis=0)
    grad_middle = grad_out + norm_back(grad_normed_two * mlp_full, middle, scale_two)
    grad_attn_low = grad_middle.astype(jnp.bfloat16)
    out_grad = jnp.einsum("nq,nd->qd", attended, grad_attn_low, preferred_element_type=jnp.float32)
    grad_mixed = jnp.einsum(
        "nd,qd->nq", grad_attn_low, out_back, preferred_element_type=jnp.float32
    ).astype(jnp.bfloat16)
    grad_mixed_seq = grad_mixed.reshape(seq_count, seq_rows, HK, groups, HD)

    def backward_head(inputs):
        grouped, keys_head, values_head, grad_head, lse = inputs
        scores = score_block(grouped, keys_head, allowed, scale)
        prob_full = jnp.exp(scores - lse)
        grad_prob = jnp.einsum(
            "qgd,sd->gqs", grad_head, values_head, preferred_element_type=jnp.float32
        )
        delta_row = jnp.sum(prob_full * grad_prob, axis=-1, keepdims=True)
        grad_scores = (prob_full * (grad_prob - delta_row)).astype(jnp.bfloat16)
        grad_query_head = (
            jnp.einsum("gqs,sd->qgd", grad_scores, keys_head, preferred_element_type=jnp.float32)
            * scale
        )
        grad_key_head = (
            jnp.einsum("gqs,qgd->sd", grad_scores, grouped, preferred_element_type=jnp.float32)
            * scale
        )
        grad_value_head = jnp.einsum(
            "gqs,qgd->sd",
            prob_full.astype(jnp.bfloat16),
            grad_head,
            preferred_element_type=jnp.float32,
        )
        return (grad_query_head, grad_key_head, grad_value_head)

    seq_item = 0
    grouped_head, keys_head, values_head = gathered[seq_item]
    grad_head = jnp.transpose(grad_mixed_seq[seq_item], (1, 0, 2, 3))
    grad_query_head, grad_key_head, grad_value_head = lax.map(
        backward_head, (grouped_head, keys_head, values_head, grad_head, lse_parts[seq_item])
    )
    grad_query_parts = jnp.transpose(grad_query_head, (1, 0, 2, 3)).reshape(seq_rows, HQ, HD)
    grad_keys_all = jnp.transpose(grad_key_head, (1, 0, 2)).reshape(-1, HK * HD)
    grad_values_all = jnp.transpose(grad_value_head, (1, 0, 2)).reshape(-1, HK * HD)
    grad_key_own = lax.psum_scatter(
        grad_keys_all.astype(jnp.bfloat16), "ctx", scatter_dimension=0, tiled=True
    ).astype(jnp.float32)
    grad_value_own = lax.psum_scatter(
        grad_values_all.astype(jnp.bfloat16), "ctx", scatter_dimension=0, tiled=True
    )
    grad_key = grad_key_own.reshape(total_rows, HK, HD)
    grad_query_unit = unrotate(grad_query_parts, cosine, sine_table)
    qgain_local = jnp.sum(grad_query_unit * query_unit, axis=(0, 1))
    grad_query_low = (
        norm_back(grad_query_unit * query_full, query_raw, query_scale)
        .astype(jnp.bfloat16)
        .reshape(total_rows, HQ * HD)
    )
    grad_key_unit = unrotate(grad_key, cosine, sine_table)
    kgain_local = jnp.sum(grad_key_unit * key_unit, axis=(0, 1))
    grad_key_low = (
        norm_back(grad_key_unit * key_full, key_raw, key_scale)
        .astype(jnp.bfloat16)
        .reshape(total_rows, HK * HD)
    )
    query_grad = jnp.einsum("nd,nc->dc", normed, grad_query_low, preferred_element_type=jnp.float32)
    key_grad = jnp.einsum("nd,nc->dc", normed, grad_key_low, preferred_element_type=jnp.float32)
    value_grad = jnp.einsum("nd,nc->dc", normed, grad_value_own, preferred_element_type=jnp.float32)
    grad_normed = jnp.einsum(
        "nc,dc->nd", grad_query_low, query_back, preferred_element_type=jnp.float32
    )
    grad_normed = grad_normed + jnp.einsum(
        "nc,dc->nd", grad_key_low, key_back, preferred_element_type=jnp.float32
    )
    grad_normed = grad_normed + jnp.einsum(
        "nc,dc->nd", grad_value_own, value_back, preferred_element_type=jnp.float32
    )
    attn_local = jnp.sum(grad_normed * flat * scale_one, axis=0)
    input_grad = grad_middle + norm_back(grad_normed * attn_full, flat, scale_one)
    shares = (
        lax.psum_scatter(
            attn_local.astype(jnp.bfloat16), "fsdp", scatter_dimension=0, tiled=True
        ).astype(jnp.float32),
        lax.psum_scatter(
            query_grad.astype(jnp.bfloat16), "fsdp", scatter_dimension=0, tiled=True
        ).astype(jnp.float32),
        lax.psum_scatter(
            key_grad.astype(jnp.bfloat16), "fsdp", scatter_dimension=0, tiled=True
        ).astype(jnp.float32),
        lax.psum_scatter(
            value_grad.astype(jnp.bfloat16), "fsdp", scatter_dimension=0, tiled=True
        ).astype(jnp.float32),
        lax.psum_scatter(
            qgain_local.astype(jnp.bfloat16), "fsdp", scatter_dimension=0, tiled=True
        ).astype(jnp.float32),
        lax.psum_scatter(
            kgain_local.astype(jnp.bfloat16), "fsdp", scatter_dimension=0, tiled=True
        ).astype(jnp.float32),
        lax.psum_scatter(
            out_grad.astype(jnp.bfloat16), "fsdp", scatter_dimension=0, tiled=True
        ).astype(jnp.float32),
        lax.psum_scatter(
            mlp_local.astype(jnp.bfloat16), "fsdp", scatter_dimension=0, tiled=True
        ).astype(jnp.float32),
        lax.psum_scatter(
            gate_grad.astype(jnp.bfloat16), "fsdp", scatter_dimension=0, tiled=True
        ).astype(jnp.float32),
        lax.psum_scatter(
            up_grad.astype(jnp.bfloat16), "fsdp", scatter_dimension=0, tiled=True
        ).astype(jnp.float32),
        lax.psum_scatter(
            down_grad.astype(jnp.bfloat16), "fsdp", scatter_dimension=0, tiled=True
        ).astype(jnp.float32),
    )
    summed = (
        lax.psum(shares[0].astype(jnp.bfloat16), "ctx").astype(jnp.float32),
        lax.psum(shares[1].astype(jnp.bfloat16), "ctx").astype(jnp.float32),
        lax.psum(shares[2].astype(jnp.bfloat16), "ctx").astype(jnp.float32),
        lax.psum(shares[3].astype(jnp.bfloat16), "ctx").astype(jnp.float32),
        lax.psum(shares[4].astype(jnp.bfloat16), "ctx").astype(jnp.float32),
        lax.psum(shares[5].astype(jnp.bfloat16), "ctx").astype(jnp.float32),
        lax.psum(shares[6].astype(jnp.bfloat16), "ctx").astype(jnp.float32),
        lax.psum(shares[7].astype(jnp.bfloat16), "ctx").astype(jnp.float32),
        lax.psum(shares[8].astype(jnp.bfloat16), "ctx").astype(jnp.float32),
        lax.psum(shares[9].astype(jnp.bfloat16), "ctx").astype(jnp.float32),
        lax.psum(shares[10].astype(jnp.bfloat16), "ctx").astype(jnp.float32),
    )
    return (
        result.reshape(tokens.shape),
        input_grad.reshape(tokens.shape),
        summed[0],
        summed[1],
        summed[2],
        summed[3],
        summed[4],
        summed[5],
        summed[6],
        summed[7],
        summed[8],
        summed[9],
        summed[10],
    )


def solution(mesh):
    placed = (
        P("fsdp", "ctx", None),
        P("fsdp", "ctx", None),
        P(),
        P("fsdp", "ctx"),
        P("fsdp"),
        P("fsdp", None),
        P("fsdp", None),
        P("fsdp", None),
        P("fsdp"),
        P("fsdp"),
        P("fsdp", None),
        P("fsdp"),
        P("fsdp", None),
        P("fsdp", None),
        P("fsdp", None),
    )
    return jax.shard_map(
        body,
        mesh=mesh,
        in_specs=placed,
        out_specs=(
            P("fsdp", "ctx", None),
            P("fsdp", "ctx", None),
            P("fsdp"),
            P("fsdp", None),
            P("fsdp", None),
            P("fsdp", None),
            P("fsdp"),
            P("fsdp"),
            P("fsdp", None),
            P("fsdp"),
            P("fsdp", None),
            P("fsdp", None),
            P("fsdp", None),
        ),
        check_vma=False,
    )
```

profile of v0, /device:TPU:0, one launch (start us, length us, event | category | flops | bytes accessed | tf_op | source)
XLA Modules:
  0.0 1395.1 jit_solution(1668268153577276082)
XLA Ops:
  13.0 6.0 all-gather
  19.8 15.7 %all-gather.12.cloned.1.call-done = bf16[1024,1024]{1,0:T(8,128)(2,1)} async-done(((bf16[256,1024]{1,0:T(8,128)(2,1)}), bf16[1024,1024]{1,0:T(8,128)(2,1)}) %all-gather.12.cloned.1.call-update) | async-done | bytes 2097168 | tf_op jit(solution)/shard_map/all_gather | solution.py:90
  35.5 3.1 convolution_convert_fusion.8
  40.5 5.9 all-reduce.6
  46.9 13.3 all-gather.16.cloned.1.call-done
  60.2 2.9 copy.56
  67.9 3.6 convert_element_type.237
  71.5 3.4 convert_element_type.238
  75.0 3.3 convert_element_type.240
  79.8 5.5 all-gather.1
  85.3 11.6 all-gather.20.cloned.1.call-done
  96.9 6.4 copy.57
  103.3 3.6 multiply_reduce_fusion.2
  111.3 61.6 %all-gather.14.cloned.1.call-done = bf16[2048,1024]{1,0:T(8,128)(2,1)} async-done(((bf16[256,1024]{1,0:T(8,128)(2,1)}), bf16[2048,1024]{1,0:T(8,128)(2,1)}) %all-gather.14.cloned.1.call-update) | async-done | bytes 4194320 | tf_op jit(solution)/shard_map/all_gather | solution.py:132
  172.9 5.2 copy.88
  178.1 6.9 copy.60
  185.1 63.1 %all-gather.18.cloned.1.call-done = bf16[2048,1024]{0,1:T(8,128)(2,1)} async-done(((bf16[256,1024]{0,1:T(8,128)(2,1)}), bf16[2048,1024]{0,1:T(8,128)(2,1)}) %all-gather.18.cloned.1.call-update) | async-done | bytes 4194320 | tf_op jit(solution)/shard_map/all_gather | solution.py:131
  248.1 6.5 copy.61
  254.6 43.6 %while.30 = (s32[]{:T(128)}, bf16[8,256,2,128]{1,3,2,0:T(8,128)(2,1)}, f32[8,2,256,1]{2,1,3,0:T(2,128)S(1)}, bf16[8,2048,128]{1,2,0:T(8,128)(2,1)}, bf16[8,2048,...) while((s32[]{:T(128)}, ...), condition=%wide.region_6.7_spmd.clone.clone, body=%wide.region_3.6_spmd.clone.sunk.clone | while | flops 545783296 | bytes 15101025 | solution.py:136
  257.5 2.6 fusion.176
  268.4 2.6 fusion.176
  279.2 2.6 fusion.176
  290.0 2.6 fusion.176
  295.6 2.6 fusion.176
  298.2 3.9 multiply_reduce_fusion.7
  303.2 28.1 %all-gather.24.cloned.1.call-done = bf16[1024,3072]{1,0:T(8,128)(2,1)} async-done(((bf16[256,3072]{1,0:T(8,128)(2,1)}), bf16[1024,3072]{1,0:T(8,128)(2,1)}) %all-gather.24.cloned.1.call-update) | async-done | bytes 6291472 | tf_op jit(solution)/shard_map/all_gather | solution.py:143
  331.4 6.2 fusion.96
  337.6 42.3 %all-gather.26.cloned.1.call-done = bf16[1024,3072]{1,0:T(8,128)(2,1)} async-done(((bf16[256,3072]{1,0:T(8,128)(2,1)}), bf16[1024,3072]{1,0:T(8,128)(2,1)}) %all-gather.26.cloned.1.call-update) | async-done | bytes 6291472 | tf_op jit(solution)/shard_map/all_gather | solution.py:144
  379.9 6.2 fusion.97
  386.2 42.3 %all-gather.28.cloned.1.call-done = bf16[3072,1024]{1,0:T(8,128)(2,1)} async-done(((bf16[768,1024]{1,0:T(8,128)(2,1)}), bf16[3072,1024]{1,0:T(8,128)(2,1)}) %all-gather.28.cloned.1.call-update) | async-done | bytes 6291472 | tf_op jit(solution)/shard_map/all_gather | solution.py:145
  428.5 9.7 multiply_convert_fusion
  438.2 5.8 fusion.98
  450.0 2.6 squeeze_reshape.11
  455.1 5.0 bitcast_bitcast_fusion
  460.1 123.0 %while.31 = (s32[]{:T(128)}, f32[8,256,2,128]{1,3,2,0:T(8,128)}, bf16[8,2048,128]{1,2,0:T(8,128)(2,1)}, bf16[8,2048,128]{1,2,0:T(8,128)(2,1)}, bf16[8,2048,128]{...) while((s32[]{:T(128)}, f32[8,256,2,128]{1,3,2,0:T(8,128)}, ...), condition=%wide.region_11.12_spmd.clone.clone, body=%wide.region_9.11_spmd.clone.sunk.clone | while | flops 1352728064 | bytes 55336092 | solution.py:218
  471.9 3.8 fusion.191
  487.2 3.8 fusion.191
  502.6 3.8 fusion.191
  517.9 3.8 fusion.191
  533.3 3.8 fusion.191
  548.7 3.8 fusion.191
  564.0 3.8 fusion.191
  579.4 3.8 fusion.191
  590.0 3.5 convolution_convert_fusion.4
  595.1 3.2 convolution_convert_fusion.3
  598.4 73.2 %reduce-scatter.10.cloned.1.call-done = bf16[256,1024]{0,1:T(8,128)(2,1)} async-done(((bf16[2048,1024]{0,1:T(8,128)(2,1)}), bf16[256,1024]{0,1:T(8,128)(2,1)}) %reduce-scatter.10.cloned.1.call-update) | async-done | bytes 524304 | tf_op jit(solution)/shard_map/reduce_scatter | solution.py:224
  676.4 87.4 %reduce-scatter.12.cloned.1.call-done = bf16[256,1024]{0,1:T(8,128)(2,1)} async-done(((bf16[2048,1024]{0,1:T(8,128)(2,1)}), bf16[256,1024]{0,1:T(8,128)(2,1)}) %reduce-scatter.12.cloned.1.call-update) | async-done | bytes 524304 | tf_op jit(solution)/shard_map/reduce_scatter | solution.py:227
  763.7 3.2 convolution_convert_fusion.6
  767.0 6.3 convolution_convert_fusion.2
  773.4 6.4 convolution_convert_fusion.1
  780.8 5.9 convolution_convert_fusion
  786.9 23.6 %reduce-scatter.14.cloned.1.call-done = bf16[256,2048]{1,0:T(8,128)(2,1)} async-done(((bf16[1024,2048]{1,0:T(8,128)(2,1)}), bf16[256,2048]{1,0:T(8,128)(2,1)}) %reduce-scatter.14.cloned.1.call-update) | async-done | bytes 1048592 | tf_op jit(solution)/shard_map/reduce_scatter | solution.py:263
  810.4 47.2 %reduce-scatter.20.cloned.1.call-done = bf16[512,1024]{1,0:T(8,128)(2,1)} async-done(((bf16[2048,1024]{1,0:T(8,128)(2,1)}), bf16[512,1024]{1,0:T(8,128)(2,1)}) %reduce-scatter.20.cloned.1.call-update) | async-done | bytes 1048592 | tf_op jit(solution)/shard_map/reduce_scatter | solution.py:278
  857.6 34.4 %reduce-scatter.16.cloned.1.call-done = bf16[256,1024]{1,0:T(8,128)(2,1)} async-done(((bf16[1024,1024]{1,0:T(8,128)(2,1)}), bf16[256,1024]{1,0:T(8,128)(2,1)}) %reduce-scatter.16.cloned.1.call-update) | async-done | bytes 524304 | tf_op jit(solution)/shard_map/reduce_scatter | solution.py:266
  892.1 34.6 %reduce-scatter.18.cloned.1.call-done = bf16[256,1024]{1,0:T(8,128)(2,1)} async-done(((bf16[1024,1024]{1,0:T(8,128)(2,1)}), bf16[256,1024]{1,0:T(8,128)(2,1)}) %reduce-scatter.18.cloned.1.call-update) | async-done | bytes 524304 | tf_op jit(solution)/shard_map/reduce_scatter | solution.py:269
  926.7 60.8 %reduce-scatter.22.cloned.1.call-done = bf16[256,3072]{1,0:T(8,128)(2,1)} async-done(((bf16[1024,3072]{1,0:T(8,128)(2,1)}), bf16[256,3072]{1,0:T(8,128)(2,1)}) %reduce-scatter.22.cloned.1.call-update) | async-done | bytes 1572880 | tf_op jit(solution)/shard_map/reduce_scatter | solution.py:284
  987.5 60.9 %reduce-scatter.24.cloned.1.call-done = bf16[256,3072]{1,0:T(8,128)(2,1)} async-done(((bf16[1024,3072]{1,0:T(8,128)(2,1)}), bf16[256,3072]{1,0:T(8,128)(2,1)}) %reduce-scatter.24.cloned.1.call-update) | async-done | bytes 1572880 | tf_op jit(solution)/shard_map/reduce_scatter | solution.py:287
  1048.4 60.8 %reduce-scatter.26.cloned.1.call-done = bf16[768,1024]{1,0:T(8,128)(2,1)} async-done(((bf16[3072,1024]{1,0:T(8,128)(2,1)}), bf16[768,1024]{1,0:T(8,128)(2,1)}) %reduce-scatter.26.cloned.1.call-update) | async-done | bytes 1572880 | tf_op jit(solution)/shard_map/reduce_scatter | solution.py:290
  1110.5 4.0 fusion.99
  1114.5 5.7 fusion.57
  1123.8 6.1 all-reduce.9
  1130.2 22.5 %all-reduce.7 = (bf16[256]{0:T(256)(128)(2,1)S(1)}, bf16[32]{0:T(256)(128)(2,1)S(1)}, bf16[32]{0:T(256)(128)(2,1)S(1)}, bf16[256]{0:T(256)(128)(2,1)S(1)}) all-reduce(bf16[256]{0:T(256)(128)(2,1)S(1)} %dynamic-slice.3, bf16[32]{0:T(256)(128)(2,1)S(1)} %dynamic-slice.5, ...), channel_id=1, replica_groups=mesh['ctx'=8,'fsdp'=4] {'ctx'}, use_global_device_ids=true, to_apply=%region_19.20 | all-reduce | flops 576 | bytes 2304 | tf_op jit(solution)/shard_map/psum | solution.py:295
  1156.1 219.2 %all-reduce.12.cloned.1.call-done = (bf16[256,2048]{1,0:T(8,128)(2,1)}, bf16[256,1024]{1,0:T(8,128)(2,1)}, bf16[256,1024]{1,0:T(8,128)(2,1)}, bf16[512,1024]{1,0...) async-done(((bf16[256,2048]{1,0:T(8,128)(2,1)}, bf16[256,1024]{1,0:T(8,128)(2,1)}, bf16[256,1024]{1,0:T(8,128)(2,1)}, ...) | async-done | bytes 7864336 | tf_op jit(solution)/shard_map/psum | solution.py:296
  1375.4 2.9 convert_element_type.256
  (326 shorter events, 182.3 us)
Async XLA Ops:
  7.2 4.6 copy-start.19
  7.2 28.3 %all-gather.12.cloned.1.call-start = ((), (), s32[]{:S(2)}) async-start(), calls=%async_computation.9 | async-start | bytes 2621440 | tf_op jit(solution)/shard_map/all_gather | solution.py:90
  9.5 3.5 copy-start.39
  9.5 9.5 copy-start.1
  9.5 50.7 %all-gather.16.cloned.1.call-start = ((), (), s32[]{:S(2)}) async-start(), calls=%async_computation.11 | async-start | bytes 2621440 | tf_op jit(solution)/shard_map/all_gather | solution.py:89
  11.7 85.2 %all-gather.20.cloned.1.call-start = ((), (), s32[]{:S(2)}) async-start(), calls=%async_computation.13 | async-start | bytes 5242880 | tf_op jit(solution)/shard_map/all_gather | solution.py:88
  12.9 25.8 %copy-start.42 = (s32[1,256]{1,0:T(1,128)S(1)}, s32[1,256]{1,0:T(1,128)}, u32[]{:S(2)}) copy-start(s32[1,256]{1,0:T(1,128)} %param.22) | copy-start | bytes 3076
  12.9 25.8 %copy-start.38 = (u32[32]{0:T(128)S(1)}, u32[32]{0:T(128)}, u32[]{:S(2)}) copy-start(u32[32]{0:T(128)} %constant.92) | copy-start | bytes 388
  12.9 27.1 %copy-start.45 = (f32[32]{0:T(128)S(1)}, f32[32]{0:T(128)}, u32[]{:S(2)}) copy-start(f32[32]{0:T(128)} %param.28) | copy-start | bytes 388
  12.9 27.3 %copy-start.46 = (f32[32]{0:T(128)S(1)}, f32[32]{0:T(128)}, u32[]{:S(2)}) copy-start(f32[32]{0:T(128)} %param.27) | copy-start | bytes 388
  12.9 159.9 %all-gather.14.cloned.1.call-start = ((), (), s32[]{:S(2)}) async-start(), calls=%async_computation.10 | async-start | bytes 4718592 | tf_op jit(solution)/shard_map/all_gather | solution.py:132
  38.6 209.5 %all-gather.18.cloned.1.call-start = ((), (), s32[]{:S(2)}) async-start(), calls=%async_computation.12 | async-start | bytes 4718592 | tf_op jit(solution)/shard_map/all_gather | solution.py:131
  46.3 18.6 %copy-start.35 = (f32[128]{0:T(128)}, f32[128]{0:T(128)S(1)}, u32[]{:S(2)}) copy-start(f32[128]{0:T(128)S(1)} %get-tuple-element.248) | copy-start | bytes 1540
  63.9 2.1 copy-start.3
  64.9 1.8 copy-start.20
  66.1 232.1 %all-gather.22.cloned.1.call-start = ((), (), s32[]{:S(2)}) async-start(), calls=%async_computation.14 | async-start | bytes 5242880 | tf_op jit(solution)/shard_map/all_gather | solution.py:91
  67.8 263.5 %all-gather.24.cloned.1.call-start = ((), (), s32[]{:S(2)}) async-start(), calls=%async_computation.15 | async-start | bytes 7864320 | tf_op jit(solution)/shard_map/all_gather | solution.py:143
  71.5 308.4 %all-gather.26.cloned.1.call-start = ((), (), s32[]{:S(2)}) async-start(), calls=%async_computation.16 | async-start | bytes 7864320 | tf_op jit(solution)/shard_map/all_gather | solution.py:144
  74.9 4.5 copy-start.40
  74.9 4.9 copy-start.41
  74.9 353.5 %all-gather.28.cloned.1.call-start = ((), (), s32[]{:S(2)}) async-start(), calls=%async_computation.17 | async-start | bytes 7864320 | tf_op jit(solution)/shard_map/all_gather | solution.py:145
  78.3 593.3 %reduce-scatter.10.cloned.1.call-start = ((), (), s32[]{:S(2)}) async-start(), calls=%async_computation.18 | async-start | bytes 4718592 | tf_op jit(solution)/shard_map/reduce_scatter | solution.py:224
  303.2 76.7 %copy-start.11 = (bf16[256,1024]{1,0:T(8,128)(2,1)}, bf16[256,1024]{1,0:T(8,128)(2,1)S(1)}, u32[]{:S(2)}) copy-start(bf16[256,1024]{1,0:T(8,128)(2,1)S(1)} %multiply_convert_fusion.3) | copy-start | bytes 1572868
  337.6 90.9 %copy-start.21 = (bf16[1,256,1024]{2,1,0:T(8,128)(2,1)S(1)}, bf16[1,256,1024]{2,1,0:T(8,128)(2,1)}, u32[]{:S(2)}) copy-start(bf16[1,256,1024]{2,1,0:T(8,128)(2,1)} %param.20) | copy-start | bytes 1572868
  438.2 5.8 copy-start.25
  438.2 5.8 copy-start.24
  438.2 5.8 copy-start.14
  438.2 6.0 copy-start.43
  444.3 3.5 copy-start.44
  465.0 2.0 copy-start
  480.3 2.0 copy-start
  495.7 2.0 copy-start
  511.0 2.0 copy-start
  526.4 2.0 copy-start
  541.8 2.0 copy-start
  557.1 2.0 copy-start
  572.5 2.0 copy-start
  583.2 180.6 %reduce-scatter.12.cloned.1.call-start = ((), (), s32[]{:S(2)}) async-start(), calls=%async_computation.19 | async-start | bytes 4718592 | tf_op jit(solution)/shard_map/reduce_scatter | solution.py:227
  583.9 226.5 %reduce-scatter.14.cloned.1.call-start = ((), (), s32[]{:S(2)}) async-start(), calls=%async_computation.20 | async-start | bytes 5242880 | tf_op jit(solution)/shard_map/reduce_scatter | solution.py:263
  588.4 1.6 copy-start.2
  593.6 264.1 %reduce-scatter.20.cloned.1.call-start = ((), (), s32[]{:S(2)}) async-start(), calls=%async_computation.23 | async-start | bytes 5242880 | tf_op jit(solution)/shard_map/reduce_scatter | solution.py:278
  598.3 74.6 %copy-start.4 = (f32[256,8,128]{0,2,1:T(8,128)S(1)}, f32[256,8,128]{0,2,1:T(8,128)}, u32[]{:S(2)}) copy-start(f32[256,8,128]{0,2,1:T(8,128)} %copy-done.3) | copy-start | bytes 3145732
  598.3 74.6 %copy-start.33 = (f32[256,8]{0,1:T(8,128)S(1)}, f32[256,8]{0,1:T(8,128)}, u32[]{:S(2)}) copy-start(f32[256,8]{0,1:T(8,128)} %copy-done.32) | copy-start | bytes 24580
  598.3 74.6 %copy-start.36 = (f32[128]{0:T(128)S(1)}, f32[128]{0:T(128)}, u32[]{:S(2)}) copy-start(f32[128]{0:T(128)} %copy-done.35) | copy-start | bytes 1540
  598.4 75.1 %copy-start.34 = (f32[256,8]{0,1:T(8,128)S(1)}, f32[256,8]{0,1:T(8,128)}, u32[]{:S(2)}) copy-start(f32[256,8]{0,1:T(8,128)} %get-tuple-element.285) | copy-start | bytes 24580
  598.4 293.7 %reduce-scatter.16.cloned.1.call-start = ((), (), s32[]{:S(2)}) async-start(), calls=%async_computation.21 | async-start | bytes 2621440 | tf_op jit(solution)/shard_map/reduce_scatter | solution.py:266
  676.0 91.0 %copy-start.12 = (bf16[256,1024]{1,0:T(8,128)(2,1)S(1)}, bf16[256,1024]{1,0:T(8,128)(2,1)}, u32[]{:S(2)}) copy-start(bf16[256,1024]{1,0:T(8,128)(2,1)} %copy-done.11) | copy-start | bytes 1572868
  676.1 250.6 %reduce-scatter.18.cloned.1.call-start = ((), (), s32[]{:S(2)}) async-start(), calls=%async_computation.22 | async-start | bytes 2621440 | tf_op jit(solution)/shard_map/reduce_scatter | solution.py:269
  767.0 220.5 %reduce-scatter.22.cloned.1.call-start = ((), (), s32[]{:S(2)}) async-start(), calls=%async_computation.24 | async-start | bytes 7864320 | tf_op jit(solution)/shard_map/reduce_scatter | solution.py:284
  773.3 275.0 %reduce-scatter.24.cloned.1.call-start = ((), (), s32[]{:S(2)}) async-start(), calls=%async_computation.25 | async-start | bytes 7864320 | tf_op jit(solution)/shard_map/reduce_scatter | solution.py:287
  779.8 329.4 %reduce-scatter.26.cloned.1.call-start = ((), (), s32[]{:S(2)}) async-start(), calls=%async_computation.26 | async-start | bytes 7864320 | tf_op jit(solution)/shard_map/reduce_scatter | solution.py:290
  786.8 588.5 %all-reduce.12.cloned.1.call-start = ((), (), s32[]{:S(2)}) async-start(), calls=%async_computation.27 | async-start | bytes 15728640 | tf_op jit(solution)/shard_map/psum | solution.py:296
  1110.5 4.0 copy-start.15
  1110.5 4.0 copy-start.17
  1114.5 5.8 copy-start.8
  1120.3 2.2 copy-start.18
  1120.3 2.4 copy-start.23
  1122.7 32.1 %copy-start.37 = (f32[256]{0:T(256)S(1)}, f32[256]{0:T(256)}, u32[]{:S(2)}) copy-start(f32[256]{0:T(256)} %get-tuple-element.287) | copy-start | bytes 3076
  1375.4 2.9 copy-start.31
  1375.4 4.0 copy-start.30
  1375.4 5.1 copy-start.29
  1378.3 3.8 copy-start.28
  1382.0 2.0 copy-start.27
  1384.1 2.0 copy-start.26
  (9 other events, 11.1 us)
Sparse Core Ops, SparseCore 0:
  10.2 25.2 all-gather.11
  37.6 22.5 all-gather.15
  62.4 34.4 all-gather.19
  99.5 73.3 all-gather.13
  174.8 73.2 all-gather.17
  250.1 32.6 all-gather.21
  284.9 46.3 all-gather.23
  333.5 46.3 all-gather.25
  382.1 46.3 all-gather.27
  583.3 88.2 reduce-scatter.9
  675.7 88.0 reduce-scatter.11
  766.1 44.2 reduce-scatter.13
  813.1 44.4 reduce-scatter.19
  860.6 31.4 reduce-scatter.15
  895.2 31.4 reduce-scatter.17
  929.1 58.3 reduce-scatter.21
  990.0 58.3 reduce-scatter.23
  1050.8 58.3 reduce-scatter.25
  1115.5 259.8 all-reduce.11
where the time goes:
time: 1400 us
  waiting for transfers between devices  981 us (70%)
  matrix products  216 us (15%)
  local copies, waits for them, and re-layouts  70.1 us (5%)
  other arithmetic  63.2 us (5%)
  blocking collectives  46 us (3%)
  between operations  17 us (1%)
    psum x1, waiting for transfers between devices, body(): lax.psum(shares[1].astype(jnp.bfloat16), 'ctx').astype(jnp.float32)  219 us
    reduce_scatter x1, waiting for transfers between devices, body(): lax.psum_scatter(grad_values_all.astype(jnp.bfloat16), 'ctx', scatter_dim...  87.4 us
    reduce_scatter x1, waiting for transfers between devices, body(): lax.psum_scatter(grad_keys_all.astype(jnp.bfloat16), 'ctx', scatter_dimen...  73.2 us
    all_gather x1, waiting for transfers between devices, body(): keys_all = lax.all_gather(key_seq[seq_item], 'ctx', axis=0, tiled=True)  63.1 us
    all_gather x1, waiting for transfers between devices, body(): values_all = lax.all_gather(value_seq[seq_item], 'ctx', axis=0, tiled=True)  61.6 us
    reduce_scatter x1, waiting for transfers between devices, body(): lax.psum_scatter(up_grad.astype(jnp.bfloat16), 'fsdp', scatter_dimension=...  60.9 us
    reduce_scatter x1, waiting for transfers between devices, body(): lax.psum_scatter(down_grad.astype(jnp.bfloat16), 'fsdp', scatter_dimensio...  60.8 us
    reduce_scatter x1, waiting for transfers between devices, body(): lax.psum_scatter(gate_grad.astype(jnp.bfloat16), 'fsdp', scatter_dimensio...  60.8 us
  transfers between devices with their start and end apart: 19, of which 18 were waited for; matrix products, arithmetic and copies ran while one was open for 12% of the time, Pallas kernels for 0%

commit v1 on v0

--- a/solution.py
+++ b/solution.py
@@ -3,6 +3,8 @@
 import jax
 import jax.numpy as jnp
 from jax import lax
+from jax.experimental import pallas as pl
+from jax.experimental.pallas import tpu as pltpu
 from jax.sharding import PartitionSpec as P
 
 D = 1024
@@ -321,6 +323,995 @@
     )
 
 
+MESH = pl.DeviceIdType.MESH
+TILE = 128
+
+
+def coords():
+    a = lax.axis_index("ctx")
+    f = lax.axis_index("fsdp")
+    return lax.div(a, 2), lax.rem(a, 2), lax.div(f, 2), lax.rem(f, 2)
+
+
+def device(z, x, y, c):
+    return (z * 2 + x, y * 2 + c)
+
+
+def both(p, q):
+    if p is None:
+        return q
+    if q is None:
+        return p
+    return jnp.logical_and(p, q)
+
+
+def guarded(p, fn):
+    if p is None:
+        fn()
+    else:
+        pl.when(p)(fn)
+
+
+class Edge:
+    def __init__(self, src, dst, to, frm, send_if=None, recv_if=None, after=()):
+        self.src, self.dst, self.to, self.frm = src, dst, to, frm
+        self.send_if, self.recv_if, self.after = send_if, recv_if, after
+
+
+def run_edges(edges, locals_, send_sems, recv_sems, local_sems):
+    barrier = pltpu.get_barrier_semaphore()
+    for e in edges:
+        guarded(
+            e.recv_if,
+            lambda e=e: pl.semaphore_signal(barrier, inc=1, device_id=e.frm, device_id_type=MESH),
+        )
+    copies = []
+    for i, (src, dst, cond) in enumerate(locals_):
+        cp = pltpu.make_async_copy(src, dst, local_sems.at[i])
+        guarded(cond, cp.start)
+        copies.append((cp, cond))
+    greeted = sum(1 if e.send_if is None else e.send_if.astype(jnp.int32) for e in edges)
+    if any(e.send_if is None for e in edges):
+        pl.semaphore_wait(barrier, greeted)
+    else:
+        pl.when(greeted > 0)(lambda: pl.semaphore_wait(barrier, greeted))
+    remote = [
+        pltpu.make_async_remote_copy(
+            src_ref=e.src,
+            dst_ref=e.dst,
+            send_sem=send_sems.at[i],
+            recv_sem=recv_sems.at[i],
+            device_id=e.to,
+            device_id_type=MESH,
+        )
+        for i, e in enumerate(edges)
+    ]
+    waited = set()
+    for i, e in enumerate(edges):
+        if not e.after:
+            guarded(e.send_if, remote[i].start)
+    for i, e in enumerate(edges):
+        for j in e.after:
+            if j not in waited:
+                guarded(edges[j].recv_if, remote[j].wait_recv)
+                waited.add(j)
+        if e.after:
+            guarded(e.send_if, remote[i].start)
+    for i, e in enumerate(edges):
+        if i not in waited:
+            guarded(e.recv_if, remote[i].wait_recv)
+        guarded(e.send_if, remote[i].wait_send)
+    for cp, cond in copies:
+        guarded(cond, cp.wait)
+
+
+def comm_call(name, cid, build, n_edges, n_locals, ins, outs):
+    def kernel(*refs):
+        i_refs, o_refs = refs[: len(ins)], refs[len(ins) : len(ins) + len(outs)]
+        send_sems, recv_sems, local_sems = refs[len(ins) + len(outs) :]
+        edges, locals_ = build(i_refs, o_refs)
+        assert len(edges) == n_edges and len(locals_) == n_locals
+        run_edges(edges, locals_, send_sems, recv_sems, local_sems)
+
+    return pl.pallas_call(
+        kernel,
+        name=name,
+        out_shape=outs,
+        in_specs=[pl.BlockSpec(memory_space=pl.ANY)] * len(ins),
+        out_specs=[pl.BlockSpec(memory_space=pl.ANY)] * len(outs),
+        scratch_shapes=[
+            pltpu.SemaphoreType.DMA((n_edges,)),
+            pltpu.SemaphoreType.DMA((n_edges,)),
+            pltpu.SemaphoreType.DMA((max(n_locals, 1),)),
+        ],
+        compiler_params=pltpu.CompilerParams(collective_id=cid, has_side_effects=True),
+    )(*ins)
+
+
+def shape(dims, dtype):
+    return jax.ShapeDtypeStruct(dims, dtype)
+
+
+def seq_partner(z, x, y, c):
+    return device(2 * c + y, x, lax.rem(z, 2), lax.div(z, 2))
+
+
+def spread(tok, cot, pos, gains, wqkv, wgu, wo, wd):
+    ins = (tok, cot, pos, gains, wqkv, wgu, wo, wd)
+    bf = jnp.bfloat16
+    outs = [
+        shape(tok.shape, bf),
+        shape(cot.shape, bf),
+        shape((4,) + pos.shape, jnp.float32),
+        shape((4,) + gains.shape, jnp.float32),
+        shape(wqkv.shape, bf),
+        shape(wgu.shape, bf),
+        shape(wo.shape, bf),
+        shape(wd.shape, bf),
+    ]
+
+    def build(i, o):
+        z, x, y, c = coords()
+        f = 2 * y + c
+        t = 2 * y + x
+        stays = z == 2 * c + y
+        moves = jnp.logical_not(stays)
+        mate = seq_partner(z, x, y, c)
+        core = device(z, x, y, 1 - c)
+        flip_y = device(z, x, 1 - y, c)
+        edges, locals_ = [], []
+
+        def slab(w, r):
+            locals_.append((w.at[t], r.at[f], None))
+            edges.append(Edge(w.at[2 * (1 - y) + x], r.at[f], flip_y, flip_y))
+            k = len(edges) - 1
+            got = r.at[2 * (1 - y) + c]
+            edges.append(Edge(w.at[t], r.at[f], core, core))
+            return (got, core, k)
+
+        relay = [slab(i[4], o[4])]
+        edges.append(Edge(i[0], o[0], mate, mate, moves, moves))
+        locals_.append((i[0], o[0], stays))
+        slot = 2 * lax.rem(z, 2) + x
+        for dy in range(2):
+            for dx in range(2):
+                xt = x if dx == 0 else 1 - x
+                yt = lax.rem(z, 2) if dy == 0 else 1 - lax.rem(z, 2)
+                to = device(2 * c + y, xt, yt, lax.div(z, 2))
+                xs = x if dx == 0 else 1 - x
+                ys = lax.rem(z, 2)
+                zs = 2 * c + (y if dy == 0 else 1 - y)
+                frm = device(zs, xs, ys, lax.div(z, 2))
+                if dx == 0 and dy == 0:
+                    edges.append(Edge(i[2], o[2].at[slot], to, frm, moves, moves))
+                    locals_.append((i[2], o[2].at[slot], stays))
+                else:
+                    edges.append(Edge(i[2], o[2].at[slot], to, frm))
+        locals_.append((i[3], o[3].at[f], None))
+        for to in (core, flip_y, device(z, x, 1 - y, 1 - c)):
+            edges.append(Edge(i[3], o[3].at[f], to, to))
+        relay.append(slab(i[5], o[5]))
+        edges.append(Edge(i[1], o[1], mate, mate, moves, moves))
+        locals_.append((i[1], o[1], stays))
+        own = c == x
+        for k in (6, 7):
+            locals_.append((i[k], o[k], own))
+            edges.append(Edge(i[k], o[k], core, core, own, jnp.logical_not(own)))
+        for got, to, k in relay:
+            edges.append(Edge(got, got, to, to, after=(k,)))
+        return edges, locals_
+
+    return comm_call("spread", 0, build, 17, 8, ins, outs)
+
+
+def core_swap(name, cid, pairs, ins, outs):
+    def build(i, o):
+        z, x, y, c = coords()
+        core = device(z, x, y, 1 - c)
+        sends, keeps = pairs(c)
+        edges = [Edge(i[a].at[s], o[b].at[d], core, core) for a, s, b, d in sends]
+        locals_ = [(i[a].at[s], o[b].at[d], None) for a, s, b, d in keeps]
+        return edges, locals_
+
+    n = [len(v) for v in pairs(0)]
+    return comm_call(name, cid, build, n[0], n[1], ins, outs)
+
+
+def plane_gather(name, cid, blocks):
+    n_in = len(blocks)
+    half = blocks[0].shape[0] // 2
+
+    def kernel(*refs):
+        i_refs, o_refs = refs[:n_in], refs[n_in : 2 * n_in]
+        send_sems, recv_sems, local_sems = refs[2 * n_in :]
+        z, x, y, c = coords()
+        me, sx, sy = 2 * y + x, 2 * y + 1 - x, 2 * (1 - y) + x
+        to_x, to_y = device(z, 1 - x, y, c), device(z, x, 1 - y, c)
+        lo, hi = pl.ds(0, half), pl.ds(half, half)
+        barrier = pltpu.get_barrier_semaphore()
+        for d in (to_x, to_y):
+            pl.semaphore_signal(barrier, inc=1, device_id=d, device_id_type=MESH)
+        keep = [
+            pltpu.make_async_copy(a, b.at[me], local_sems.at[k])
+            for k, (a, b) in enumerate(zip(i_refs, o_refs))
+        ]
+        for cp in keep:
+            cp.start()
+        pl.semaphore_wait(barrier, 2)
+
+        def copy(k, j, src, dst, to):
+            return pltpu.make_async_remote_copy(
+                src_ref=src,
+                dst_ref=dst,
+                send_sem=send_sems.at[k, j],
+                recv_sem=recv_sems.at[k, j],
+                device_id=to,
+                device_id_type=MESH,
+            )
+
+        all_copies = []
+        for k, (a, b) in enumerate(zip(i_refs, o_refs)):
+            cps = [
+                copy(k, 0, a.at[lo], b.at[me, lo], to_x),
+                copy(k, 1, a.at[hi], b.at[me, hi], to_y),
+                copy(k, 2, a.at[hi], b.at[me, hi], to_x),
+                copy(k, 3, a.at[lo], b.at[me, lo], to_y),
+                copy(k, 4, b.at[sy, hi], b.at[sy, hi], to_x),
+                copy(k, 5, b.at[sx, lo], b.at[sx, lo], to_y),
+            ]
+            for cp in cps[:4]:
+                cp.start()
+            all_copies.append(cps)
+        for cps in all_copies:
+            cps[1].wait_recv()
+            cps[4].start()
+            cps[0].wait_recv()
+            cps[5].start()
+        for cps in all_copies:
+            for j in (2, 3, 4, 5):
+                cps[j].wait_recv()
+            for cp in cps:
+                cp.wait_send()
+        for cp in keep:
+            cp.wait()
+
+    return pl.pallas_call(
+        kernel,
+        name=name,
+        out_shape=[shape((4,) + b.shape, b.dtype) for b in blocks],
+        in_specs=[pl.BlockSpec(memory_space=pl.ANY)] * n_in,
+        out_specs=[pl.BlockSpec(memory_space=pl.ANY)] * n_in,
+        scratch_shapes=[
+            pltpu.SemaphoreType.DMA((n_in, 6)),
+            pltpu.SemaphoreType.DMA((n_in, 6)),
+            pltpu.SemaphoreType.DMA((n_in,)),
+        ],
+        compiler_params=pltpu.CompilerParams(collective_id=cid, has_side_effects=True),
+    )(*blocks)
+
+
+def plane_scatter(name, cid, partials):
+    n_in = len(partials)
+    rows, cols = partials[0].shape[1:]
+    half = rows // 2
+
+    def kernel(*refs):
+        i_refs, o_refs = refs[:n_in], refs[n_in : 2 * n_in]
+        got, mid, send_sems, recv_sems = refs[2 * n_in :]
+        z, x, y, c = coords()
+        me, sx, sy, sd = 2 * y + x, 2 * y + 1 - x, 2 * (1 - y) + x, 2 * (1 - y) + 1 - x
+        to_x, to_y = device(z, 1 - x, y, c), device(z, x, 1 - y, c)
+        lo, hi = pl.ds(0, half), pl.ds(half, half)
+        barrier = pltpu.get_barrier_semaphore()
+        for d in (to_x, to_y):
+            pl.semaphore_signal(barrier, inc=1, device_id=d, device_id_type=MESH)
+        pl.semaphore_wait(barrier, 2)
+
+        def copy(k, j, src, to):
+            return pltpu.make_async_remote_copy(
+                src_ref=src,
+                dst_ref=got.at[k, j],
+                send_sem=send_sems.at[k, j],
+                recv_sem=recv_sems.at[k, j],
+                device_id=to,
+                device_id_type=MESH,
+            )
+
+        every = []
+        for k, a in enumerate(i_refs):
+            cps = [
+                copy(k, 0, a.at[sd, lo], to_x),
+                copy(k, 1, a.at[sd, hi], to_y),
+                copy(k, 2, a.at[sx, lo], to_x),
+                copy(k, 3, a.at[sy, hi], to_y),
+                copy(k, 4, mid.at[k, 0], to_x),
+                copy(k, 5, mid.at[k, 1], to_y),
+            ]
+            for cp in cps[:4]:
+                cp.start()
+            every.append(cps)
+        f32, bf = jnp.float32, jnp.bfloat16
+        for k, a in enumerate(i_refs):
+            cps = every[k]
+            cps[0].wait_recv()
+            mid[k, 1] = (a[sy, lo].astype(f32) + got[k, 0].astype(f32)).astype(bf)
+            cps[5].start()
+            cps[1].wait_recv()
+            mid[k, 0] = (a[sx, hi].astype(f32) + got[k, 1].astype(f32)).astype(bf)
+            cps[4].start()
+        for k, (a, b) in enumerate(zip(i_refs, o_refs)):
+            cps = every[k]
+            for j in (2, 3, 4, 5):
+                cps[j].wait_recv()
+            b[lo] = a[me, lo].astype(f32) + got[k, 2].astype(f32) + got[k, 5].astype(f32)
+            b[hi] = a[me, hi].astype(f32) + got[k, 3].astype(f32) + got[k, 4].astype(f32)
+            for cp in cps:
+                cp.wait_send()
+
+    vm = pl.BlockSpec(memory_space=pltpu.VMEM)
+    return pl.pallas_call(
+        kernel,
+        name=name,
+        out_shape=[shape((rows, cols), jnp.float32) for _ in partials],
+        in_specs=[vm] * n_in,
+        out_specs=[vm] * n_in,
+        scratch_shapes=[
+            pltpu.VMEM((n_in, 6, half, cols), jnp.bfloat16),
+            pltpu.VMEM((n_in, 2, half, cols), jnp.bfloat16),
+            pltpu.SemaphoreType.DMA((n_in, 6)),
+            pltpu.SemaphoreType.DMA((n_in, 6)),
+        ],
+        compiler_params=pltpu.CompilerParams(
+            collective_id=cid, has_side_effects=True, vmem_limit_bytes=40 * 2**20
+        ),
+    )(*partials)
+
+
+QT = 256
+NEG = -1e30
+
+
+def dot_nt(a, b):
+    return lax.dot_general(a, b, (((1,), (1,)), ((), ())), preferred_element_type=jnp.float32)
+
+
+def dot_tn(a, b):
+    return lax.dot_general(a, b, (((0,), (0,)), ((), ())), preferred_element_type=jnp.float32)
+
+
+def dot_nn(a, b):
+    return jnp.dot(a, b, preferred_element_type=jnp.float32)
+
+
+LOG2E = math.log2(math.e)
+
+
+def attend_forward(inverse, qkv):
+    length = qkv.shape[0]
+    tiles = length // QT
+    blocks = QT // BLK
+    factor = HD ** (-0.5) * LOG2E
+
+    def kernel(inv, x_ref, o_ref, lse_ref, q_s, k_s, v_s):
+        @pl.loop(0, tiles)
+        def _(i):
+            for h in range(blocks):
+                s = inv[i * blocks + h]
+                rows = pl.ds(pl.multiple_of(s * BLK, BLK), BLK)
+                at = pl.multiple_of(i * QT, QT) + h * BLK
+                q_s[i, pl.ds(h * BLK, BLK), :] = x_ref[rows, 0:HD]
+                q_s[i, pl.ds(QT + h * BLK, BLK), :] = x_ref[rows, HD : 2 * HD]
+                k_s[pl.ds(at, BLK), :] = x_ref[rows, 2 * HD : 3 * HD]
+                v_s[pl.ds(at, BLK), 0:HD] = x_ref[rows, 3 * HD : 4 * HD]
+        v_s[:, HD : 2 * HD] = jnp.ones((length, HD), jnp.bfloat16)
+        rows_ = lax.broadcasted_iota(jnp.int32, (2 * QT, QT), 0)
+        cols_ = lax.broadcasted_iota(jnp.int32, (2 * QT, QT), 1)
+        allowed = jnp.where(rows_ >= QT, rows_ - QT, rows_) >= cols_
+
+        @pl.loop(0, tiles)
+        def _(i):
+            q = q_s[i]
+
+            def step(j, acc):
+                at = pl.ds(pl.multiple_of(j * QT, QT), QT)
+                p = jnp.exp2(dot_nt(q, k_s[at, :]) * factor).astype(jnp.bfloat16)
+                return acc + dot_nn(p, v_s[at, :])
+
+            acc = lax.fori_loop(0, i, step, jnp.zeros((2 * QT, 2 * HD), jnp.float32))
+            at = pl.ds(pl.multiple_of(i * QT, QT), QT)
+            scores = jnp.where(allowed, dot_nt(q, k_s[at, :]) * factor, NEG)
+            acc = acc + dot_nn(jnp.exp2(scores).astype(jnp.bfloat16), v_s[at, :])
+            total = acc[:, HD:]
+            out = acc[:, :HD] / total
+            lse_ref[i] = jnp.log2(jnp.transpose(total)[0:8, :])
+            for h in range(blocks):
+                s = inv[i * blocks + h]
+                rows = pl.ds(pl.multiple_of(s * BLK, BLK), BLK)
+                o_ref[rows, 0:HD] = out[h * BLK : (h + 1) * BLK].astype(jnp.bfloat16)
+                o_ref[rows, HD : 2 * HD] = out[QT + h * BLK : QT + (h + 1) * BLK].astype(
+                    jnp.bfloat16
+                )
+
+    vm = pl.BlockSpec(memory_space=pltpu.VMEM)
+    return pl.pallas_call(
+        kernel,
+        name="attend_forward",
+        out_shape=[
+            shape((length, 2 * HD), jnp.bfloat16),
+            shape((tiles, 8, 2 * QT), jnp.float32),
+        ],
+        in_specs=[pl.BlockSpec(memory_space=pltpu.SMEM), vm],
+        out_specs=[vm, vm],
+        scratch_shapes=[
+            pltpu.VMEM((tiles, 2 * QT, HD), jnp.bfloat16),
+            pltpu.VMEM((length, HD), jnp.bfloat16),
+            pltpu.VMEM((length, 2 * HD), jnp.bfloat16),
+        ],
+        compiler_params=pltpu.CompilerParams(vmem_limit_bytes=40 * 2**20),
+        cost_estimate=pl.CostEstimate(
+            flops=2 * 2 * 2 * length * length * HD, bytes_accessed=4 * 2**20, transcendentals=0
+        ),
+    )(inverse, qkv)
+
+
+def attend_backward(inverse, qkv, mixed, grad, lse):
+    length = qkv.shape[0]
+    tiles = length // QT
+    blocks = QT // BLK
+    scale = HD ** (-0.5)
+    factor = scale * LOG2E
+
+    def kernel(inv, x_ref, o_ref, g_ref, lse_ref, d_ref, q_s, g_s, k_s, v_s, delta_s, dq_s):
+        @pl.loop(0, tiles)
+        def _(i):
+            for h in range(blocks):
+                s = inv[i * blocks + h]
+                rows = pl.ds(pl.multiple_of(s * BLK, BLK), BLK)
+                at = pl.ds(pl.multiple_of(i * QT, QT) + h * BLK, BLK)
+                for u in range(2):
+                    to = pl.ds(u * QT + h * BLK, BLK)
+                    lanes = slice(u * HD, (u + 1) * HD)
+                    q_s[i, to, :] = x_ref[rows, lanes]
+                    g_s[i, to, :] = g_ref[rows, lanes]
+                    product = g_ref[rows, lanes].astype(jnp.float32) * o_ref[
+                        rows, lanes
+                    ].astype(jnp.float32)
+                    delta_s[i, :, to] = jnp.broadcast_to(
+                        jnp.sum(jnp.transpose(product), axis=0, keepdims=True), (8, BLK)
+                    )
+                k_s[at, :] = x_ref[rows, 2 * HD : 3 * HD]
+                v_s[at, :] = x_ref[rows, 3 * HD : 4 * HD]
+        dq_s[...] = jnp.zeros_like(dq_s)
+        rows_ = lax.broadcasted_iota(jnp.int32, (QT, 2 * QT), 0)
+        cols_ = lax.broadcasted_iota(jnp.int32, (QT, 2 * QT), 1)
+        allowed = jnp.where(cols_ >= QT, cols_ - QT, cols_) >= rows_
+
+        @pl.loop(0, tiles)
+        def _(j):
+            at = pl.ds(pl.multiple_of(j * QT, QT), QT)
+            k, v = k_s[at, :], v_s[at, :]
+
+            def pair(i, carry, diagonal):
+                dk, dv = carry
+                q, g = q_s[i], g_s[i]
+                scores = dot_nt(k, q) * factor - lse_ref[i, 0:1, :]
+                if diagonal:
+                    scores = jnp.where(allowed, scores, NEG)
+                p = jnp.exp2(scores)
+                ds = (p * (dot_nt(v, g) - delta_s[i, 0:1, :])).astype(jnp.bfloat16)
+                dq_s[i] += dot_tn(ds, k)
+                return (dk + dot_nn(ds, q), dv + dot_nn(p.astype(jnp.bfloat16), g))
+
+            zero = jnp.zeros((QT, HD), jnp.float32)
+            carry = pair(j, (zero, zero), True)
+            dk, dv = lax.fori_loop(j + 1, tiles, lambda i, cr: pair(i, cr, False), carry)
+            for h in range(blocks):
+                s = inv[j * blocks + h]
+                rows = pl.ds(pl.multiple_of(s * BLK, BLK), BLK)
+                part = slice(h * BLK, (h + 1) * BLK)
+                d_ref[rows, 2 * HD : 3 * HD] = (dk[part] * scale).astype(jnp.bfloat16)
+                d_ref[rows, 3 * HD : 4 * HD] = dv[part].astype(jnp.bfloat16)
+
+        @pl.loop(0, tiles)
+        def _(i):
+            for h in range(blocks):
+                s = inv[i * blocks + h]
+                rows = pl.ds(pl.multiple_of(s * BLK, BLK), BLK)
+                for u in range(2):
+                    d_ref[rows, u * HD : (u + 1) * HD] = (
+                        dq_s[i, pl.ds(u * QT + h * BLK, BLK), :] * scale
+                    ).astype(jnp.bfloat16)
+
+    vm = pl.BlockSpec(memory_space=pltpu.VMEM)
+    return pl.pallas_call(
+        kernel,
+        name="attend_backward",
+        out_shape=shape((length, 4 * HD), jnp.bfloat16),
+        in_specs=[pl.BlockSpec(memory_space=pltpu.SMEM), vm, vm, vm, vm],
+        out_specs=vm,
+        scratch_shapes=[
+            pltpu.VMEM((tiles, 2 * QT, HD), jnp.bfloat16),
+            pltpu.VMEM((tiles, 2 * QT, HD), jnp.bfloat16),
+            pltpu.VMEM((length, HD), jnp.bfloat16),
+            pltpu.VMEM((length, HD), jnp.bfloat16),
+            pltpu.VMEM((tiles, 8, 2 * QT), jnp.float32),
+            pltpu.VMEM((tiles, 2 * QT, HD), jnp.float32),
+        ],
+        compiler_params=pltpu.CompilerParams(vmem_limit_bytes=40 * 2**20),
+        cost_estimate=pl.CostEstimate(
+            flops=5 * 2 * 2 * length * length * HD, bytes_accessed=8 * 2**20, transcendentals=0
+        ),
+    )(inverse, qkv, mixed, grad, lse)
+
+
+def line_sum(name, cid, own, lag=4):
+    tiles, rows, cols = own.shape
+    depth = lax.axis_size("ctx") // 2
+    root = depth // 2
+
+    def kernel(a, mine, other, low, high, part, s_sem, r_sem):
+        z, x, y, c = coords()
+        flip_x = device(z, 1 - x, y, c)
+        up, down = device(z + 1, x, y, c), device(z - 1, x, y, c)
+        has_down, has_up = z > 0, z < depth - 1
+        below, above, is_root = z < root, z > root, z == root
+        barrier = pltpu.get_barrier_semaphore()
+
+        def signal(to):
+            pl.semaphore_signal(barrier, inc=1, device_id=to, device_id_type=MESH)
+
+        signal(flip_x)
+        pl.when(has_down)(lambda: signal(down))
+        pl.when(has_up)(lambda: signal(up))
+        pl.semaphore_wait(barrier, 1 + has_down.astype(jnp.int32) + has_up.astype(jnp.int32))
+
+        def copy(kind, k, src, dst, to):
+            return pltpu.make_async_remote_copy(
+                src_ref=src,
+                dst_ref=dst.at[k],
+                send_sem=s_sem.at[kind, k],
+                recv_sem=r_sem.at[kind, k],
+                device_id=to,
+                device_id_type=MESH,
+            )
+
+        def up_part(k):
+            return copy(0, k, part.at[k], low, up)
+
+        def down_part(k):
+            return copy(1, k, part.at[k], high, down)
+
+        def down_sum(k):
+            return copy(2, k, mine.at[k], mine, down)
+
+        def up_sum(k):
+            return copy(3, k, mine.at[k], mine, up)
+
+        def x_sum(k):
+            return copy(4, k, mine.at[k], other, flip_x)
+
+        f32, bf = jnp.float32, jnp.bfloat16
+
+        def gather(k):
+            @pl.when(below)
+            def _():
+                @pl.when(has_down)
+                def _():
+                    up_part(k).wait_recv()
+                    part[k] = (a[k].astype(f32) + low[k].astype(f32)).astype(bf)
+
+                @pl.when(jnp.logical_not(has_down))
+                def _():
+                    part[k] = a[k]
+
+                up_part(k).start()
+
+            @pl.when(above)
+            def _():
+                @pl.when(has_up)
+                def _():
+                    down_part(k).wait_recv()
+                    part[k] = (a[k].astype(f32) + high[k].astype(f32)).astype(bf)
+
+                @pl.when(jnp.logical_not(has_up))
+                def _():
+                    part[k] = a[k]
+
+                down_part(k).start()
+
+        def finish(k):
+            @pl.when(is_root)
+            def _():
+                up_part(k).wait_recv()
+                total = a[k].astype(f32) + low[k].astype(f32)
+                if root < depth - 1:
+                    down_part(k).wait_recv()
+                    total = total + high[k].astype(f32)
+                mine[k] = total.astype(bf)
+                down_sum(k).start()
+                if root < depth - 1:
+                    up_sum(k).start()
+
+            @pl.when(below)
+            def _():
+                down_sum(k).wait_recv()
+                pl.when(has_down)(lambda: down_sum(k).start())
+
+            @pl.when(above)
+            def _():
+                up_sum(k).wait_recv()
+                pl.when(has_up)(lambda: up_sum(k).start())
+
+            x_sum(k).start()
+
+        is_end = jnp.logical_or(z == 0, z == depth - 1)
+        behind = jnp.where(is_end, tiles, lag)
+
+        @pl.loop(0, 2 * tiles)
+        def _(k):
+            pl.when(k < tiles)(lambda: gather(k))
+            pl.when(jnp.logical_and(k >= behind, k < tiles + behind))(lambda: finish(k - behind))
+
+        @pl.loop(0, tiles)
+        def _(k):
+            pl.when(below)(lambda: up_part(k).wait_send())
+            pl.when(above)(lambda: down_part(k).wait_send())
+            pl.when(jnp.logical_and(has_down, jnp.logical_not(above)))(
+                lambda: down_sum(k).wait_send()
+            )
+            pl.when(jnp.logical_and(has_up, jnp.logical_not(below)))(
+                lambda: up_sum(k).wait_send()
+            )
+            x_sum(k).wait()
+
+    vm = pl.BlockSpec(memory_space=pltpu.VMEM)
+    bf = jnp.bfloat16
+    return pl.pallas_call(
+        kernel,
+        name=name,
+        out_shape=[shape(own.shape, bf), shape(own.shape, bf)],
+        in_specs=[vm],
+        out_specs=[vm, vm],
+        scratch_shapes=[
+            pltpu.VMEM(own.shape, bf),
+            pltpu.VMEM(own.shape, bf),
+            pltpu.VMEM(own.shape, bf),
+            pltpu.SemaphoreType.DMA((5, tiles)),
+            pltpu.SemaphoreType.DMA((5, tiles)),
+        ],
+        compiler_params=pltpu.CompilerParams(
+            collective_id=cid, has_side_effects=True, vmem_limit_bytes=56 * 2**20
+        ),
+    )(own)
+
+
+def fast_body(
+    tokens,
+    cotangent,
+    block_map,
+    positions,
+    attn_gain,
+    query_weight,
+    key_weight,
+    value_weight,
+    query_gain,
+    key_gain,
+    out_weight,
+    mlp_gain,
+    gate_weight,
+    up_weight,
+    down_weight,
+):
+    bf, f32 = jnp.bfloat16, jnp.float32
+    z, x, y, c = coords()
+    rows = tokens.shape[1]
+    d_rows = query_weight.shape[0]
+    ff = gate_weight.shape[1]
+    unit = ff // 4
+    wqkv = jnp.concatenate(
+        [
+            query_weight.astype(bf).reshape(d_rows, 8, 2 * HD),
+            key_weight.astype(bf).reshape(d_rows, 8, HD),
+            value_weight.astype(bf).reshape(d_rows, 8, HD),
+        ],
+        axis=-1,
+    ).reshape(d_rows, 4, 8 * HD)
+    wqkv = jnp.transpose(wqkv, (1, 0, 2))
+    wgu = jnp.concatenate(
+        [
+            gate_weight.astype(bf).reshape(d_rows, 4, unit),
+            up_weight.astype(bf).reshape(d_rows, 4, unit),
+        ],
+        axis=-1,
+    )
+    wgu = jnp.transpose(wgu, (1, 0, 2))
+    gains = jnp.concatenate([attn_gain, mlp_gain, query_gain, key_gain])
+    n_gain = gains.shape[0]
+    gains = jnp.pad(gains, (0, 1024 - n_gain)).reshape(8, 128)
+    pos = jnp.pad(positions.reshape(-1).astype(f32), (0, 1024 - rows)).reshape(8, 128)
+    tok, cot, pos_all, gains_all, wqkv, wgu, wo, wd = spread(
+        tokens.reshape(rows, D),
+        cotangent.reshape(rows, D),
+        pos,
+        gains,
+        wqkv,
+        wgu,
+        out_weight.astype(bf),
+        down_weight.astype(bf),
+    )
+    wqkv = wqkv.reshape(D, 8 * HD)
+    wgu = wgu.reshape(D, 2 * unit)
+    flat_gains = gains_all.reshape(4, 1024)
+    attn_full = flat_gains[:, :d_rows].reshape(-1)
+    mlp_full = flat_gains[:, d_rows : 2 * d_rows].reshape(-1)
+    hd = HD // 4
+    query_full = flat_gains[:, 2 * d_rows : 2 * d_rows + hd].reshape(-1)
+    key_full = flat_gains[:, 2 * d_rows + hd : 2 * d_rows + 2 * hd].reshape(-1)
+    pos_rows = pos_all.reshape(4, 1024)[:, :rows].reshape(-1)
+
+    flat = tok.astype(f32)
+    scale_one = rms_scale(flat)
+    n1_own = (flat * scale_one * attn_full).astype(bf)
+    n1, dy = plane_gather("gather_n1", 1, [n1_own, cot])
+    n1, dy = n1.reshape(-1, D), dy.reshape(-1, D)
+    half = n1.shape[0]
+    raw = jnp.dot(n1, wqkv, preferred_element_type=f32).reshape(half, 2, 4, HD)
+    cosine, sine = rope_tables(pos_rows, HD)
+    cosine, sine = cosine[:, None, None, :], sine[:, None, None, :]
+    qk_raw = raw[:, :, :3]
+    qk_scale = rms_scale(qk_raw)
+    qk_unit = qk_raw * qk_scale
+    qk_gain = jnp.stack([query_full, query_full, key_full])
+    qk = rotate(qk_unit * qk_gain, cosine, sine).astype(bf)
+    qkv = jnp.concatenate([qk, raw[:, :, 3:].astype(bf)], axis=2).reshape(half, 2, 4 * HD)
+    qkv = jnp.transpose(qkv, (1, 0, 2))
+
+    (qkv_core,) = core_swap(
+        "swap_qkv",
+        2,
+        lambda c: (
+            [(0, 1 - c, 0, c)],
+            [(0, c, 0, c)],
+        ),
+        (qkv,),
+        [shape((2, half, 4 * HD), bf)],
+    )
+    qkv_core = qkv_core.reshape(2 * half, 4 * HD)
+    inverse = jnp.argsort(block_map.reshape(-1)).astype(jnp.int32)
+    mixed, lse = attend_forward(inverse, qkv_core)
+    mixed2 = mixed.reshape(2, half, 2 * HD)
+
+    (attended,) = core_swap(
+        "swap_mixed",
+        3,
+        lambda c: ([(0, 1 - c, 0, c)], [(0, c, 0, c)]),
+        (mixed2,),
+        [shape((2, half, 2 * HD), bf)],
+    )
+    attended = jnp.concatenate([attended[0], attended[1]], axis=-1)
+    part = jnp.dot(attended, wo, preferred_element_type=f32).astype(bf).reshape(4, rows, D)
+    (delta,) = plane_scatter("scatter_out", 4, [part])
+    middle = flat + delta
+    scale_two = rms_scale(middle)
+    n2_own = (middle * scale_two * mlp_full).astype(bf)
+    (n2,) = plane_gather("gather_n2", 5, [n2_own])
+    n2 = n2.reshape(-1, D)
+    gate_up = jnp.dot(n2, wgu, preferred_element_type=f32)
+    gate, upward = gate_up[:, :unit], gate_up[:, unit:]
+    sigmoid_gate = jax.nn.sigmoid(gate)
+    silu_gate = gate * sigmoid_gate
+    hidden = (silu_gate * upward).astype(bf)
+    result_part = jnp.dot(hidden, wd, preferred_element_type=f32).astype(bf).reshape(4, rows, D)
+    grad_hidden = lax.dot_general(
+        dy, wd, (((1,), (1,)), ((), ())), preferred_element_type=f32
+    )
+    grad_gate = (grad_hidden * upward * sigmoid_gate * (1.0 + gate * (1.0 - sigmoid_gate))).astype(
+        bf
+    )
+    grad_up = (grad_hidden * silu_gate).astype(bf)
+    grad_gu = jnp.concatenate([grad_gate, grad_up], axis=-1)
+    dn2_part = (
+        lax.dot_general(grad_gu, wgu, (((1,), (1,)), ((), ())), preferred_element_type=f32)
+        .astype(bf)
+        .reshape(4, rows, D)
+    )
+    grad_normed_two, result_add = plane_scatter("scatter_mlp", 6, [dn2_part, result_part])
+    result = middle + result_add
+    grad_out = cot.astype(f32)
+    mlp_local = jnp.sum(grad_normed_two * middle * scale_two, axis=0)
+    grad_middle = grad_out + norm_back(grad_normed_two * mlp_full, middle, scale_two)
+    (dmb,) = plane_gather("gather_dmiddle", 7, [grad_middle.astype(bf)])
+    dmb = dmb.reshape(-1, D)
+    grad_mixed = lax.dot_general(
+        dmb, wo, (((1,), (1,)), ((), ())), preferred_element_type=f32
+    ).astype(bf)
+    (grad_core,) = core_swap(
+        "swap_grad_mixed",
+        8,
+        lambda c: ([(0, 1 - c, 0, c)], [(0, c, 0, c)]),
+        (jnp.stack([grad_mixed[:, : 2 * HD], grad_mixed[:, 2 * HD :]]),),
+        [shape((2, half, 2 * HD), bf)],
+    )
+    grad_core = grad_core.reshape(2 * half, 2 * HD)
+    dqkv_core = attend_backward(inverse, qkv_core, mixed, grad_core, lse)
+    (dqkv,) = core_swap(
+        "swap_dqkv",
+        9,
+        lambda c: ([(0, 1 - c, 0, c)], [(0, c, 0, c)]),
+        (dqkv_core.reshape(2, half, 4 * HD),),
+        [shape((2, half, 4 * HD), bf)],
+    )
+    dqkv = jnp.stack([dqkv[0], dqkv[1]], axis=1).reshape(half, 2, 4, HD)
+    grad_unit = unrotate(dqkv[:, :, :3].astype(f32), cosine, sine)
+    gain_local = jnp.sum(grad_unit * qk_unit, axis=(0, 1))
+    grad_qk = norm_back(grad_unit * qk_gain, qk_raw, qk_scale).astype(bf)
+    dqkv = jnp.concatenate([grad_qk, dqkv[:, :, 3:]], axis=2).reshape(half, 8 * HD)
+    dn1_part = (
+        lax.dot_general(dqkv, wqkv, (((1,), (1,)), ((), ())), preferred_element_type=f32)
+        .astype(bf)
+        .reshape(4, rows, D)
+    )
+    (grad_normed,) = plane_scatter("scatter_dn1", 10, [dn1_part])
+    attn_local = jnp.sum(grad_normed * flat * scale_one, axis=0)
+    input_grad = grad_middle + norm_back(grad_normed * attn_full, flat, scale_one)
+
+    def back(i, o):
+        z, x, y, c = coords()
+        stays = z == 2 * c + y
+        moves = jnp.logical_not(stays)
+        mate = seq_partner(z, x, y, c)
+        edges = [Edge(i[k], o[k], mate, mate, moves, moves) for k in range(2)]
+        return edges, [(i[k], o[k], stays) for k in range(2)]
+
+    result, input_grad = comm_call(
+        "outputs_back",
+        11,
+        back,
+        2,
+        2,
+        (result.astype(bf), input_grad.astype(bf)),
+        [shape((rows, D), bf)] * 2,
+    )
+
+    n_q = gain_local[0] + gain_local[1]
+    gain_sums = lax.psum(
+        jnp.concatenate([attn_local, mlp_local, n_q, gain_local[2]]), ("ctx", "fsdp")
+    )
+    f = 2 * y + c
+
+    def own_gain(at, size):
+        return lax.dynamic_slice_in_dim(gain_sums, at + f * (size // 4), size // 4)
+
+    dqkv_w = lax.dot_general(
+        n1, dqkv, (((0,), (0,)), ((), ())), preferred_element_type=f32
+    ).astype(bf)
+    dgu_w = lax.dot_general(
+        n2, grad_gu, (((0,), (0,)), ((), ())), preferred_element_type=f32
+    ).astype(bf)
+    do_w = lax.dot_general(
+        attended, dmb, (((0,), (0,)), ((), ())), preferred_element_type=f32
+    ).astype(bf)
+    dd_w = lax.dot_general(hidden, dy, (((0,), (0,)), ((), ())), preferred_element_type=f32).astype(
+        bf
+    )
+    dqkv_w = dqkv_w.reshape(4, d_rows, 8 * HD)
+    dgu_w = dgu_w.reshape(4, d_rows, 2 * unit)
+    do_w = do_w.reshape(2, -1, D)
+    dd_w = dd_w.reshape(2, -1, D)
+    ins = (dqkv_w, dgu_w, do_w, dd_w)
+    got = core_swap(
+        "swap_weight_grads",
+        12,
+        lambda c: (
+            [(k, 2 * yy + (1 - c), k, yy) for k in range(2) for yy in range(2)]
+            + [(k, 1 - c, k, slice(None)) for k in (2, 3)],
+            [],
+        ),
+        ins,
+        [
+            shape((2,) + dqkv_w.shape[1:], bf),
+            shape((2,) + dgu_w.shape[1:], bf),
+            shape(do_w.shape[1:], bf),
+            shape(dd_w.shape[1:], bf),
+        ],
+    )
+
+    def own_half(w, axis_pairs):
+        if axis_pairs:
+            w = w.reshape((2, 2) + w.shape[1:])
+            return lax.dynamic_index_in_dim(w, c, 1, keepdims=False)
+        return lax.dynamic_index_in_dim(w, c, 0, keepdims=False)
+
+    sums = [
+        (own_half(w, k < 2).astype(f32) + r.astype(f32)).astype(bf)
+        for k, (w, r) in enumerate(zip(ins, got))
+    ]
+    def y_swap(i, o):
+        z, x, y, c = coords()
+        flip = device(z, x, 1 - y, c)
+        edges = [Edge(i[k].at[1 - y], o[k].at[y], flip, flip) for k in range(2)]
+        locals_ = [(i[k].at[y], o[k].at[y], None) for k in range(2)]
+        return edges, locals_
+
+    sq, sg = comm_call(
+        "swap_rows",
+        13,
+        y_swap,
+        2,
+        2,
+        (sums[0], sums[1]),
+        [shape(sums[0].shape, bf), shape(sums[1].shape, bf)],
+    )
+    cols = 512
+
+    def to_tiles(w):
+        w = w.reshape((-1, TILE, w.shape[-1] // cols, cols))
+        return jnp.transpose(w, (0, 2, 1, 3)).reshape(-1, TILE, cols)
+
+    pieces = [to_tiles(w) for w in (sq, sg, sums[2], sums[3])]
+    mine, other = line_sum("line_sum", 14, jnp.concatenate(pieces))
+    counts = [p.shape[0] for p in pieces]
+    starts = [sum(counts[:k]) for k in range(len(counts))]
+
+    def from_tiles(tiles_, like):
+        n_rows, n_cols = like
+        w = tiles_.reshape(n_rows // TILE, n_cols // cols, TILE, cols)
+        return jnp.transpose(w, (0, 2, 1, 3)).reshape(n_rows, n_cols)
+
+    def part_of(tiles_, k):
+        return tiles_[starts[k] : starts[k] + counts[k]]
+
+    od_first = starts[2]
+    od_count = counts[2] + counts[3]
+    (od_got,) = core_swap(
+        "swap_od",
+        15,
+        lambda c: ([(0, 1 - c, 0, slice(None))], []),
+        (
+            jnp.where(
+                x == 0,
+                jnp.stack([mine[od_first:], other[od_first:]]),
+                jnp.stack([other[od_first:], mine[od_first:]]),
+            ),
+        ),
+        [shape((od_count, TILE, cols), bf)],
+    )
+    od_own = jnp.where(c == x, mine[od_first:], other[od_first:])
+    od = jnp.where(c == 0, jnp.stack([od_own, od_got]), jnp.stack([od_got, od_own]))
+    grad_o = jnp.concatenate(
+        [from_tiles(od[k, : counts[2]], do_w.shape[1:]) for k in range(2)]
+    ).astype(f32)
+    grad_d = jnp.concatenate(
+        [from_tiles(od[k, counts[2] :], dd_w.shape[1:]) for k in range(2)]
+    ).astype(f32)
+
+    def quarters(k, n_cols):
+        m = from_tiles(part_of(mine, k), (2 * d_rows, n_cols)).reshape(2, d_rows, n_cols)
+        o = from_tiles(part_of(other, k), (2 * d_rows, n_cols)).reshape(2, d_rows, n_cols)
+        first = jnp.where(x == 0, m, o)
+        second = jnp.where(x == 0, o, m)
+        q = jnp.stack([first, second], axis=1).reshape(4, d_rows, n_cols)
+        return jnp.transpose(q, (1, 0, 2)).astype(f32)
+
+    gq = quarters(0, 8 * HD).reshape(d_rows, 8, 4 * HD)
+    gg = quarters(1, 2 * unit)
+    return (
+        result.astype(f32).reshape(tokens.shape),
+        input_grad.astype(f32).reshape(tokens.shape),
+        own_gain(0, D),
+        gq[:, :, : 2 * HD].reshape(d_rows, -1),
+        gq[:, :, 2 * HD : 3 * HD].reshape(d_rows, -1),
+        gq[:, :, 3 * HD :].reshape(d_rows, -1),
+        own_gain(2 * D, HD),
+        own_gain(2 * D + HD, HD),
+        grad_o,
+        own_gain(D, D),
+        gg[:, :, :unit].reshape(d_rows, -1),
+        gg[:, :, unit:].reshape(d_rows, -1),
+        grad_d,
+    )
+
+
 def solution(mesh):
     placed = (
         P("fsdp", "ctx", None),
@@ -339,8 +1330,9 @@
         P("fsdp", None),
         P("fsdp", None),
     )
+    fits = mesh.shape["fsdp"] == 4 and mesh.shape["ctx"] == 8
     return jax.shard_map(
-        body,
+        fast_body if fits else body,
         mesh=mesh,
         in_specs=placed,
         out_specs=(

time: 1400 us -> 904 us (0.65)
  waiting for transfers between devices: 981 us -> 0 us
  Pallas kernels: 0 us -> 636 us
  matrix products: 216 us -> 43.8 us
  local copies, waits for them, and re-layouts: 70.1 us -> 108 us
  between operations: 17 us -> 2.12 us
    pallas_call x0 -> x18, Pallas kernels: none -> 636 us  [the longest x9 337 us: comm_call(): pl.pallas_call(kernel, name=name, out_shape=outs, in_specs=[pl.BlockSpec(...]
    reduce_scatter x9 -> x0, waiting for transfers between devices: 483 us -> none  [the longest x1 87.4 us: body(): lax.psum_scatter(grad_values_all.astype(jnp.bfloat16), 'ctx', scatter_dim...]
    all_gather x9 -> x0, waiting for transfers between devices: 278 us -> none  [the longest x1 63.1 us: body(): keys_all = lax.all_gather(key_seq[seq_item], 'ctx', axis=0, tiled=True)]
    psum x1 -> x0, waiting for transfers between devices: 219 us -> none  [body(): lax.psum(shares[1].astype(jnp.bfloat16), 'ctx').astype(jnp.float32)]
    dot_general x77 -> x12, matrix products: 216 us -> 43.8 us  [the longest x1 6.46 us: fast_body(): lax.dot_general(n2, grad_gu, (((0,), (0,)), ((), ())), preferred_element_...]
    reshape x1 -> x14, local copies, waits for them, and re-layouts: 0.08 us -> 26.1 us  [the longest x7 10.9 us: to_tiles(): w = w.reshape((-1, TILE, w.shape[-1] // cols, cols))]
    select_n x0 -> x10, local copies, waits for them, and re-layouts: none -> 16.7 us  [the longest x5 9.17 us: quarters(): second = jnp.where(x == 0, o, m)]
    slice x0 -> x10, local copies, waits for them, and re-layouts: none -> 15.8 us  [the longest x2 5.68 us: fast_body(): gg[:, :, unit:].reshape(d_rows, -1)]
  transfers between devices with their start and end apart: 19 -> 0, of which waited for: 18 -> 0; matrix products, arithmetic and copies ran while one was open for 12% -> 0% of each run, Pallas kernels for 0% -> 0%
where the time goes in v1:
time: 904 us; the launch traced here: 894 us
  Pallas kernels  636 us (70%)
  local copies, waits for them, and re-layouts  108 us (12%)
  other arithmetic  66.9 us (7%)
  matrix products  43.8 us (5%)
  blocking collectives  37.1 us (4%)
    pallas_call x9, Pallas kernels, comm_call(): pl.pallas_call(kernel, name=name, out_shape=outs, in_specs=[pl.BlockSpec(...  337 us
    pallas_call x1, Pallas kernels, line_sum(): pl.pallas_call(kernel, name=name, out_shape=[shape(own.shape, bf), shape(...  118 us
    pallas_call x3, Pallas kernels, plane_scatter(): pl.pallas_call(kernel, name=name, out_shape=[shape((rows, cols), jnp.floa...  68.4 us
    pallas_call x3, Pallas kernels, plane_gather(): pl.pallas_call(kernel, name=name, out_shape=[shape((4,) + b.shape, b.dtyp...  67.3 us
    psum x1, blocking collectives, fast_body(): lax.psum(jnp.concatenate([attn_local, mlp_local, n_q, gain_local[2]]), ('...  37.1 us
    unnamed x121, local copies, waits for them, and re-layouts  32.7 us
    pallas_call x1, Pallas kernels, attend_backward(): pl.pallas_call(kernel, name='attend_backward', out_shape=shape((length, 4...  27.1 us

profile of v1, /device:TPU:0, one launch (start us, length us, event | category | flops | bytes accessed | tf_op | source)
XLA Modules:
  0.0 894.3 jit_solution(8716914266602674862)
XLA Ops:
  2.7 2.2 copy.149
  5.6 3.0 copy.150
  10.4 1.9 maximum_bitcast_fusion.refs_5_
  18.8 2.4 copy.148
  21.1 3.4 convert_element_type.185.refs_7_
  25.7 152.8 %spread.1 = (bf16[256,1024]{1,0:T(8,128)(2,1)}, bf16[256,1024]{1,0:T(8,128)(2,1)}, f32[4,8,128]{2,1,0:T(8,128)}, f32[4,8,128]{2,1,0:T(8,128)}, bf16[4,256,1024]{...) custom-call(bf16[256,1024]{1,0:T(8,128)(2,1)} %bitcast.268, ...), custom_call_target="tpu_custom_call" | custom-call | tf_op jit(solution)/shard_map/spread/pallas_call | solution.py:416
  181.8 2.0 fusion.16.refs_0_
  183.8 33.1 %gather_n1.1 = (bf16[4,256,1024]{2,1,0:T(8,128)(2,1)}, bf16[4,256,1024]{2,1,0:T(8,128)(2,1)}) custom-call(bf16[256,1024]{1,0:T(8,128)(2,1)} %fusion.16.refs_0_, bf16[256,1024]{1,0:T(8,128)(2,1)} %get-tuple-element.41.refs_1_), custom_call_target="tpu_custom_call" | custom-call | tf_op jit(solution)/shard_map/gather_n1/pallas_call | solution.py:578
  216.9 2.6 copy.154
  219.5 4.6 fusion.43
  224.1 1.9 copy-done.6
  226.7 2.3 multiply_multiply_fusion
  229.8 1.9 fusion.26
  233.1 2.6 copy.188
  235.7 32.9 %swap_qkv.1 = bf16[2,1024,512]{2,1,0:T(8,128)(2,1)} custom-call(bf16[2,1024,512]{2,1,0:T(8,128)(2,1)} %bitcast.216), custom_call_target="tpu_custom_call" | custom-call | tf_op jit(solution)/shard_map/swap_qkv/pallas_call | solution.py:416
  271.6 17.7 %attend_forward.1 = (bf16[2048,256]{1,0:T(8,128)(2,1)S(1)}, f32[8,8,512]{2,1,0:T(8,128)S(1)}) custom-call(s32[16]{0:T(128)S(1)} %get-tuple-element.39.inv, bf16[2048,512]{1,0:T(8,128)(2,1)S(1)} %bitcast.195), custom_call_target="tpu_custom_call" | custom-call | flops 4294967296 | bytes 4194304 | tf_op jit(solution)/shard_map/attend_forward/pallas_call | solution.py:736
  290.3 17.0 %swap_mixed.1 = bf16[2,1024,256]{2,1,0:T(8,128)(2,1)} custom-call(bf16[2,1024,256]{2,1,0:T(8,128)(2,1)} %bitcast.200), custom_call_target="tpu_custom_call" | custom-call | tf_op jit(solution)/shard_map/swap_mixed/pallas_call | solution.py:416
  309.8 19.2 %scatter_out.1 = f32[256,1024]{1,0:T(8,128)S(1)} custom-call(bf16[4,256,1024]{2,1,0:T(8,128)(2,1)S(1)} %bitcast.194), custom_call_target="tpu_custom_call" | custom-call | tf_op jit(solution)/shard_map/scatter_out/pallas_call | solution.py:652
  330.2 17.1 %gather_n2.1 = bf16[4,256,1024]{2,1,0:T(8,128)(2,1)} custom-call(bf16[256,1024]{1,0:T(8,128)(2,1)} %multiply_convert_fusion.3.refs_0_), custom_call_target="tpu_custom_call" | custom-call | tf_op jit(solution)/shard_map/gather_n2/pallas_call | solution.py:578
  347.3 6.2 fusion.44
  353.6 3.4 multiply_convert_fusion.2
  357.0 1.9 convolution_convert_fusion.4
  360.6 4.1 fusion.11
  364.7 29.3 %scatter_mlp.1 = (f32[256,1024]{1,0:T(8,128)S(1)}, f32[256,1024]{1,0:T(8,128)S(1)}) custom-call(bf16[4,256,1024]{2,1,0:T(8,128)(2,1)S(1)} %bitcast.199, bf16[4,256,1024]{2,1,0:T(8,128)(2,1)S(1)} %bitcast.197), custom_call_target="tpu_custom_call" | custom-call | tf_op jit(solution)/shard_map/scatter_mlp/pallas_call | solution.py:652
  396.8 17.1 %gather_dmiddle.1 = bf16[4,256,1024]{2,1,0:T(8,128)(2,1)} custom-call(bf16[256,1024]{1,0:T(8,128)(2,1)} %get-tuple-element.96.refs_0_), custom_call_target="tpu_custom_call" | custom-call | tf_op jit(solution)/shard_map/gather_dmiddle/pallas_call | solution.py:578
  413.9 4.0 convolution_convert_fusion.6
  417.9 6.5 convolution_convert_fusion
  426.9 17.0 %swap_grad_mixed.1 = bf16[2,1024,256]{2,1,0:T(8,128)(2,1)} custom-call(bf16[2,1024,256]{2,1,0:T(8,128)(2,1)} %pad_maximum_fusion.10.refs_0_), custom_call_target="tpu_custom_call" | custom-call | tf_op jit(solution)/shard_map/swap_grad_mixed/pallas_call | solution.py:416
  445.1 27.1 %attend_backward.1 = bf16[2048,512]{1,0:T(8,128)(2,1)S(1)} custom-call(s32[16]{0:T(128)S(1)} %get-tuple-element.39.inv, bf16[2048,512]{1,0:T(8,128)(2,1)S(1)} %bitcast.196, bf16[2048,256]{1,0:T(8,128)(2,1)S(1)} %copy-done.4, bf16[2048,256]{1,0:T(8,128)(2,1)S(1)} %bitcast.201, f32[8,8,512]{2,1,0:T(8,128)S(1)} %get-tuple-element.52.lse_ref), custom_call_target="tpu_custom_call" | custom-call | flops 10737418240 | bytes 8388608 | tf_op jit(solution)/shard_map/attend_backward/pallas_call | solution.py:826
  473.6 32.9 %swap_dqkv.1 = bf16[2,1024,512]{2,1,0:T(8,128)(2,1)} custom-call(bf16[2,1024,512]{2,1,0:T(8,128)(2,1)} %bitcast.198), custom_call_target="tpu_custom_call" | custom-call | tf_op jit(solution)/shard_map/swap_dqkv/pallas_call | solution.py:416
  506.5 2.6 fusion.39
  516.9 2.1 copy-done.42
  519.0 3.7 convolution_convert_fusion.1
  522.8 2.9 convolution_convert_fusion.5
  525.7 7.2 swap_weight_grads.1
  533.0 3.1 fusion.5.refs_1_
  537.5 40.9 %swap_rows.1 = (bf16[2,256,1024]{2,1,0:T(8,128)(2,1)}, bf16[2,256,1536]{2,1,0:T(8,128)(2,1)}) custom-call(bf16[2,256,1024]{2,1,0:T(8,128)(2,1)} %fusion.9.refs_0_, bf16[2,256,1536]{2,1,0:T(8,128)(2,1)} %fusion.5.refs_1_), custom_call_target="tpu_custom_call" | custom-call | tf_op jit(solution)/shard_map/swap_rows/pallas_call | solution.py:416
  578.4 3.7 copy.163
  584.1 2.6 reshape.459
  589.8 1.9 copy.165
  596.0 3.7 pad_maximum_fusion.a
  599.7 118.4 %line_sum.1 = (bf16[30,128,512]{2,1,0:T(8,128)(2,1)}, bf16[30,128,512]{2,1,0:T(8,128)(2,1)}) custom-call(bf16[30,128,512]{2,1,0:T(8,128)(2,1)} %pad_maximum_fusion.a), custom_call_target="tpu_custom_call" | custom-call | tf_op jit(solution)/shard_map/line_sum/pallas_call | solution.py:969
  718.2 3.0 select_bitcast_fusion
  721.2 3.3 maximum_select_fusion.refs_0_
  724.5 3.4 swap_od.1
  728.0 2.1 maximum_select_fusion.1
  732.7 2.1 maximum_convert_fusion.1
  734.8 3.2 broadcast_select_fusion.1
  740.2 3.5 copy.175
  743.7 2.7 copy.174
  747.5 3.5 copy.176
  753.8 3.3 fusion.34
  757.1 2.4 copy.177
  759.5 2.4 copy.184
  761.9 2.4 copy.178
  764.3 2.6 copy.185
  776.7 2.3 copy.169
  778.9 5.4 copy.170
  793.0 4.0 convolution_convert_fusion.2
  797.1 19.9 %scatter_dn1.1 = f32[256,1024]{1,0:T(8,128)S(1)} custom-call(bf16[4,256,1024]{2,1,0:T(8,128)(2,1)S(1)} %bitcast.193), custom_call_target="tpu_custom_call" | custom-call | tf_op jit(solution)/shard_map/scatter_dn1/pallas_call | solution.py:652
  817.5 37.1 %psum.7 = f32[2304]{0:T(1024)S(1)} all-reduce(f32[2304]{0:T(1024)S(1)} %pad_maximum_fusion.14), channel_id=1, replica_groups=mesh['ctx'=8,'fsdp'=4] {'ctx','fsdp'}, use_global_device_ids=true, to_apply=%region_10.11 | all-reduce | flops 2304 | bytes 18432 | tf_op jit(solution)/shard_map/psum | solution.py:1177
  856.9 32.9 %outputs_back.1 = (bf16[256,1024]{1,0:T(8,128)(2,1)}, bf16[256,1024]{1,0:T(8,128)(2,1)}) custom-call(bf16[256,1024]{1,0:T(8,128)(2,1)} %get-tuple-element.126.refs_0_, bf16[256,1024]{1,0:T(8,128)(2,1)} %fusion.20.refs_1_), custom_call_target="tpu_custom_call" | custom-call | tf_op jit(solution)/shard_map/outputs_back/pallas_call | solution.py:416
  889.8 2.1 bitcast_convert_fusion
  891.9 2.1 bitcast_convert_fusion.1
  (199 shorter events, 83.5 us)
Async XLA Ops:
  10.4 2.4 copy-start.24
  12.8 1.2 copy-start.29
  21.1 3.4 copy-start.25
  178.5 38.4 %copy-start.26 = (bf16[4,256,1024]{2,1,0:T(8,128)(2,1)S(1)}, bf16[4,256,1024]{2,1,0:T(8,128)(2,1)}, u32[]{:S(2)}) copy-start(bf16[4,256,1024]{2,1,0:T(8,128)(2,1)} %get-tuple-element.43) | copy-start | bytes 6291460
  180.5 3.3 copy-start.34
  181.2 0.6 copy-start.32
  224.1 2.0 copy-start.6
  229.0 0.7 copy-start.36
  229.0 2.7 copy-start.7
  231.7 1.1 copy-start.14
  231.7 1.1 copy-start.17
  235.7 32.9 %copy-start.38 = (s32[8,2]{0,1:T(2,128)S(1)}, s32[8,2]{0,1:T(2,128)}, u32[]{:S(2)}) copy-start(s32[8,2]{0,1:T(2,128)} %param.17) | copy-start | bytes 196
  270.0 1.6 copy-start
  289.3 1.0 copy-start.3
  290.3 18.3 %copy-start.44 = (bf16[512,1024]{1,0:T(8,128)(2,1)S(1)}, bf16[512,1024]{1,0:T(8,128)(2,1)}, u32[]{:S(2)}) copy-start(bf16[512,1024]{1,0:T(8,128)(2,1)} %get-tuple-element.46) | copy-start | bytes 3145732
  309.8 19.2 %copy-start.9 = (bf16[256,1024]{1,0:T(8,128)(2,1)S(1)}, bf16[256,1024]{1,0:T(8,128)(2,1)}, u32[]{:S(2)}) copy-start(bf16[256,1024]{1,0:T(8,128)(2,1)} %get-tuple-element.38) | copy-start | bytes 1572868
  347.3 6.3 copy-start.40
  347.3 6.3 copy-start.43
  357.0 1.9 copy-start.46
  357.0 1.9 copy-start.48
  357.0 2.4 copy-start.50
  357.0 3.6 copy-start.39
  394.0 1.0 copy-start.23
  413.9 4.0 copy-start.21
  413.9 4.0 copy-start.49
  417.9 6.5 copy-start.22
  417.9 6.5 copy-start.45
  425.8 18.1 %copy-start.1 = (bf16[2,1024,512]{2,1,0:T(8,128)(2,1)S(1)}, bf16[2,1024,512]{2,1,0:T(8,128)(2,1)}, u32[]{:S(2)}) copy-start(bf16[2,1024,512]{2,1,0:T(8,128)(2,1)} %swap_qkv.1) | copy-start | bytes 6291460
  425.8 18.1 %copy-start.4 = (bf16[2048,256]{1,0:T(8,128)(2,1)S(1)}, bf16[2048,256]{1,0:T(8,128)(2,1)}, u32[]{:S(2)}) copy-start(bf16[2048,256]{1,0:T(8,128)(2,1)} %copy-done.3) | copy-start | bytes 3145732
  443.9 1.2 copy-start.5
  472.2 1.3 copy-start.2
  509.1 2.0 copy-start.18
  511.6 2.2 copy-start.8
  511.6 2.3 copy-start.15
  516.7 2.3 copy-start.42
  516.9 5.9 copy-start.28
  519.0 3.7 copy-start.41
  519.0 3.7 copy-start.47
  525.7 7.3 copy-start.12
  533.0 3.1 copy-start.16
  533.0 3.1 copy-start.30
  586.7 1.5 copy-start.20
  586.7 1.7 copy-start.31
  730.1 1.6 copy-start.11
  747.5 3.5 copy-start.13
  791.1 2.0 copy-start.27
  797.0 20.0 %copy-start.10 = (bf16[256,1024]{1,0:T(8,128)(2,1)S(1)}, bf16[256,1024]{1,0:T(8,128)(2,1)}, u32[]{:S(2)}) copy-start(bf16[256,1024]{1,0:T(8,128)(2,1)} %get-tuple-element.38) | copy-start | bytes 1572868
  797.0 20.0 %copy-start.33 = (f32[1,2,4,128]{3,1,2,0:T(2,128)S(1)}, f32[1,2,4,128]{3,1,2,0:T(2,128)}, u32[]{:S(2)}) copy-start(f32[1,2,4,128]{3,1,2,0:T(2,128)} %copy-done.32) | copy-start | bytes 12292
  797.0 20.0 %copy-start.35 = (f32[256]{0:T(256)S(1)}, f32[256]{0:T(256)}, u32[]{:S(2)}) copy-start(f32[256]{0:T(256)} %copy-done.34) | copy-start | bytes 3076
  797.0 58.7 %copy-start.19 = (f32[256,1024]{1,0:T(8,128)S(1)}, f32[256,1024]{1,0:T(8,128)}, u32[]{:S(2)}) copy-start(f32[256,1024]{1,0:T(8,128)} %get-tuple-element.97) | copy-start | bytes 3145732
  797.0 58.7 %copy-start.37 = (f32[256]{0:T(256)S(1)}, f32[256]{0:T(256)}, u32[]{:S(2)}) copy-start(f32[256]{0:T(256)} %get-tuple-element.143) | copy-start | bytes 3076

commit v2 on v0

--- a/solution.py
+++ b/solution.py
@@ -3,6 +3,8 @@
 import jax
 import jax.numpy as jnp
 from jax import lax
+from jax.experimental import pallas as pl
+from jax.experimental.pallas import tpu as pltpu
 from jax.sharding import PartitionSpec as P
 
 D = 1024
@@ -321,6 +323,1761 @@
     )
 
 
+MESH = pl.DeviceIdType.MESH
+BF = jnp.bfloat16
+F32 = jnp.float32
+LOG2E = math.log2(math.e)
+QT = 256
+NEG = -1e30
+
+
+def shape(dims, dtype):
+    return jax.ShapeDtypeStruct(dims, dtype)
+
+
+def dot_nn(a, b):
+    return jnp.dot(a, b, preferred_element_type=F32)
+
+
+def dot_nt(a, b):
+    return lax.dot_general(a, b, (((1,), (1,)), ((), ())), preferred_element_type=F32)
+
+
+def dot_tn(a, b):
+    return lax.dot_general(a, b, (((0,), (0,)), ((), ())), preferred_element_type=F32)
+
+
+def device(z, x, y, c):
+    return (z * 2 + x, y * 2 + c)
+
+
+def coords():
+    a = lax.axis_index("ctx")
+    f = lax.axis_index("fsdp")
+    return lax.div(a, 2), lax.rem(a, 2), lax.div(f, 2), lax.rem(f, 2)
+
+
+class Net:
+    def __init__(self, send_sems, recv_sems):
+        self.z, self.x, self.y, self.c = z, x, y, c = coords()
+        self.depth = lax.axis_size("ctx") // 2
+        self.to_x = device(z, 1 - x, y, c)
+        self.to_y = device(z, x, 1 - y, c)
+        self.to_core = device(z, x, y, 1 - c)
+        self.to_x_other = device(z, 1 - x, y, 1 - c)
+        self.up = device(z + 1, x, y, c)
+        self.down = device(z - 1, x, y, c)
+        self.has_up = z < self.depth - 1
+        self.has_down = z > 0
+        self.send_sems, self.recv_sems = send_sems, recv_sems
+        self.used = 0
+        self.me = 2 * y + x
+        self.sx = 2 * y + 1 - x
+        self.sy = 2 * (1 - y) + x
+        self.sd = 2 * (1 - y) + 1 - x
+
+    def greet(self, line=True, owners=False, mate=None):
+        barrier = pltpu.get_barrier_semaphore()
+
+        def signal(to):
+            pl.semaphore_signal(barrier, inc=1, device_id=to, device_id_type=MESH)
+
+        for to in (self.to_x, self.to_y, self.to_core):
+            signal(to)
+        count = 3
+        if owners:
+            signal(self.to_x_other)
+            count = count + 1
+        if mate is not None:
+            pl.when(mate[0])(lambda: signal(mate[1]))
+            count = count + mate[0].astype(jnp.int32)
+        if line:
+            pl.when(self.has_up)(lambda: signal(self.up))
+            pl.when(self.has_down)(lambda: signal(self.down))
+            count = count + self.has_up.astype(jnp.int32) + self.has_down.astype(jnp.int32)
+        pl.semaphore_wait(barrier, count)
+
+    def take(self, count=1):
+        first = self.used
+        self.used += count
+        assert self.used <= self.send_sems.shape[0], self.used
+        return first
+
+    def copy(self, sem, src, dst, to):
+        return pltpu.make_async_remote_copy(
+            src_ref=src,
+            dst_ref=dst,
+            send_sem=self.send_sems.at[sem],
+            recv_sem=self.recv_sems.at[sem],
+            device_id=to,
+            device_id_type=MESH,
+        )
+
+    def new(self, src, dst, to):
+        return self.copy(self.take(), src, dst, to)
+
+
+def rms(values):
+    return lax.rsqrt(jnp.mean(values * values, axis=-1, keepdims=True) + epsilon)
+
+
+class PlaneGather:
+    def __init__(self, net, src, out):
+        half = out.shape[1] // 2
+        lo, hi = pl.ds(0, half), pl.ds(half, half)
+        me, sx, sy = net.me, net.sx, net.sy
+        self.x_lo = net.new(src.at[lo], out.at[me, lo], net.to_x)
+        self.y_hi = net.new(src.at[hi], out.at[me, hi], net.to_y)
+        self.x_hi = net.new(src.at[hi], out.at[me, hi], net.to_x)
+        self.y_lo = net.new(src.at[lo], out.at[me, lo], net.to_y)
+        self.fx = net.new(out.at[sy, hi], out.at[sy, hi], net.to_x)
+        self.fy = net.new(out.at[sx, lo], out.at[sx, lo], net.to_y)
+
+    def start(self):
+        for cp in (self.x_lo, self.y_hi, self.x_hi, self.y_lo):
+            cp.start()
+
+    def forward(self):
+        self.y_hi.wait_recv()
+        self.fx.start()
+        self.x_lo.wait_recv()
+        self.fy.start()
+
+    def wait_sides(self):
+        self.x_hi.wait_recv()
+        self.y_lo.wait_recv()
+
+    def wait_diagonal(self):
+        self.fx.wait_recv()
+        self.fy.wait_recv()
+
+    def drain(self):
+        for cp in (self.x_lo, self.y_hi, self.x_hi, self.y_lo, self.fx, self.fy):
+            cp.wait_send()
+
+
+class PlaneSum:
+    def __init__(self, net, part, got, mid):
+        half = part.shape[1] // 2
+        self.half = half
+        self.lo, self.hi = lo, hi = pl.ds(0, half), pl.ds(half, half)
+        self.net, self.part, self.got, self.mid = net, part, got, mid
+        me, sx, sy, sd = net.me, net.sx, net.sy, net.sd
+        self.c0 = net.new(part.at[sd, lo], got.at[0], net.to_x)
+        self.c1 = net.new(part.at[sd, hi], got.at[1], net.to_y)
+        self.c2 = net.new(part.at[sx, lo], got.at[2], net.to_x)
+        self.c3 = net.new(part.at[sy, hi], got.at[3], net.to_y)
+        self.c4 = net.new(mid.at[0], got.at[4], net.to_x)
+        self.c5 = net.new(mid.at[1], got.at[5], net.to_y)
+
+    def start_diagonal(self):
+        self.c0.start()
+        self.c1.start()
+
+    def start_sides(self):
+        self.c2.start()
+        self.c3.start()
+
+    def forward(self):
+        net = self.net
+        self.c0.wait_recv()
+        self.mid[1] = (
+            self.part[net.sy, self.lo].astype(F32) + self.got[0].astype(F32)
+        ).astype(BF)
+        self.c5.start()
+        self.c1.wait_recv()
+        self.mid[0] = (
+            self.part[net.sx, self.hi].astype(F32) + self.got[1].astype(F32)
+        ).astype(BF)
+        self.c4.start()
+
+    def finish(self, use):
+        me = self.net.me
+        for rows, a, b, first, second in (
+            (self.lo, self.c2, self.c5, 2, 5),
+            (self.hi, self.c3, self.c4, 3, 4),
+        ):
+            a.wait_recv()
+            b.wait_recv()
+            use(
+                rows,
+                self.part[me, rows].astype(F32)
+                + self.got[first].astype(F32)
+                + self.got[second].astype(F32),
+            )
+
+    def drain(self):
+        for cp in (self.c0, self.c1, self.c2, self.c3, self.c4, self.c5):
+            cp.wait_send()
+
+
+class Route:
+    def __init__(self, net, src, line, out, parts=2):
+        self.net, self.src, self.line, self.out = net, src, line, out
+        self.SUB = parts
+        self.rows = src.shape[0] // self.SUB
+        depth = net.depth
+        self.l_sem = net.take(depth * self.SUB)
+        self.c_sem = net.take(2 * self.SUB)
+        self.y_sem = net.take(2 * self.SUB)
+        self.x_sem = net.take(2 * self.SUB)
+        self.place = 2 * net.c + net.y
+        self.entry = net.z == self.place
+        self.row0 = net.y == lax.rem(net.z, 2)
+
+    def part(self, s):
+        return pl.ds(s * self.rows, self.rows)
+
+    def hop(self, k, s, own, to):
+        src = self.src.at[self.part(s)] if own else self.line.at[k, self.part(s)]
+        return self.net.copy(self.l_sem + k * self.SUB + s, src, self.line.at[k, self.part(s)], to)
+
+    def chip(self, k, s):
+        j = lax.rem(k, 2)
+        return self.net.copy(
+            self.c_sem + j * self.SUB + s,
+            self.line.at[k, self.part(s)],
+            self.out.at[2 * j + self.net.x, self.part(s)],
+            self.net.to_core,
+        )
+
+    def over_y(self, j, s):
+        at = self.out.at[2 * j + self.net.x, self.part(s)]
+        return self.net.copy(self.y_sem + j * self.SUB + s, at, at, self.net.to_y)
+
+    def over_x(self, j, s):
+        at = self.out.at[2 * j + self.net.x, self.part(s)]
+        return self.net.copy(self.x_sem + j * self.SUB + s, at, at, self.net.to_x)
+
+    def from_x(self, j, s):
+        at = self.out.at[2 * j + 1 - self.net.x, self.part(s)]
+        return self.net.copy(self.x_sem + j * self.SUB + s, at, at, self.net.to_x)
+
+    def start(self):
+        net = self.net
+        for s in range(self.SUB):
+            pl.when(net.z < self.place)(lambda: self.hop(net.z, s, True, net.up).start())
+            pl.when(net.z > self.place)(lambda: self.hop(net.z, s, True, net.down).start())
+
+    def relay(self):
+        net = self.net
+        for d in range(1, net.depth):
+            for s in range(self.SUB):
+
+                @pl.when(jnp.logical_and(net.z < self.place, net.z >= d))
+                def _():
+                    self.hop(net.z - d, s, False, net.up).wait_recv()
+                    self.hop(net.z - d, s, False, net.up).start()
+
+                @pl.when(jnp.logical_and(net.z > self.place, net.z < net.depth - d))
+                def _():
+                    self.hop(net.z + d, s, False, net.down).wait_recv()
+                    self.hop(net.z + d, s, False, net.down).start()
+
+    def enter(self):
+        net = self.net
+        for d in range(net.depth):
+            for s in range(self.SUB):
+                for k in range(net.depth):
+                    near = jnp.logical_or(self.place - k == d, k - self.place == d)
+                    here = jnp.logical_and(self.entry, near)
+
+                    @pl.when(here)
+                    def _():
+                        if d > 0:
+                            self.hop(k, s, False, net.up).wait_recv()
+                        else:
+                            self.line[k, self.part(s)] = self.src[self.part(s)]
+
+                    @pl.when(jnp.logical_and(here, net.c == k // 2))
+                    def _():
+                        self.out[2 * (k % 2) + net.x, self.part(s)] = self.line[k, self.part(s)]
+                        self.over_x(k % 2, s).start()
+                        self.over_y(k % 2, s).start()
+
+                    @pl.when(jnp.logical_and(here, net.c != k // 2))
+                    def _():
+                        self.chip(k, s).start()
+
+    def spread(self):
+        net = self.net
+        beside = jnp.logical_and(self.row0, jnp.logical_not(self.entry))
+
+        def one(j, s):
+            @pl.when(beside)
+            def _():
+                self.chip(j, s).wait_recv()
+                self.over_x(j, s).start()
+                self.over_y(j, s).start()
+
+            @pl.when(jnp.logical_not(self.row0))
+            def _():
+                self.over_y(j, s).wait_recv()
+                self.over_x(j, s).start()
+
+        @pl.loop(0, 2)
+        def _(n):
+            j = jnp.where(net.z <= 2 * net.c, n, 1 - n)
+            for s in range(self.SUB):
+                one(j, s)
+
+    def wait(self, j):
+        for s in range(self.SUB):
+            self.from_x(j, s).wait_recv()
+
+    def drain(self):
+        net = self.net
+        for s in range(self.SUB):
+            pl.when(net.z < self.place)(lambda: self.hop(net.z, s, True, net.up).wait_send())
+            pl.when(net.z > self.place)(lambda: self.hop(net.z, s, True, net.down).wait_send())
+            for d in range(1, net.depth):
+
+                @pl.when(jnp.logical_and(net.z < self.place, net.z >= d))
+                def _():
+                    self.hop(net.z - d, s, False, net.up).wait_send()
+
+                @pl.when(jnp.logical_and(net.z > self.place, net.z < net.depth - d))
+                def _():
+                    self.hop(net.z + d, s, False, net.down).wait_send()
+
+            for k in range(net.depth):
+
+                @pl.when(jnp.logical_and(self.entry, net.c != k // 2))
+                def _():
+                    self.chip(k, s).wait_send()
+
+            for j in range(2):
+                self.over_x(j, s).wait_send()
+                pl.when(self.row0)(lambda: self.over_y(j, s).wait_send())
+
+
+class LineSum:
+    def __init__(self, net, tiles, src, mine, low, high, part, deliver):
+        self.net, self.tiles, self.src, self.mine = net, tiles, src, mine
+        self.low, self.high, self.part, self.deliver = low, high, part, deliver
+        self.sems = net.take(4 * tiles)
+        self.root = net.depth // 2
+        self.below = net.z < self.root
+        self.above = net.z > self.root
+        self.middle = net.z == self.root
+        self.two_sided = self.root < net.depth - 1
+
+    def hop(self, kind, k):
+        net = self.net
+        src, dst, to = (
+            (self.part.at[k], self.low.at[k], net.up),
+            (self.part.at[k], self.high.at[k], net.down),
+            (self.mine(k), self.mine(k), net.down),
+            (self.mine(k), self.mine(k), net.up),
+        )[kind]
+        return net.copy(self.sems + kind * self.tiles + k, src, dst, to)
+
+    def gather(self, k):
+        net = self.net
+
+        def send(kind, slots, has_before):
+            @pl.when(has_before)
+            def _():
+                self.hop(kind, k).wait_recv()
+                total = self.src(k)[...].astype(F32) + slots[k].astype(F32)
+                self.part[k] = total.astype(self.part.dtype)
+
+            @pl.when(jnp.logical_not(has_before))
+            def _():
+                self.part[k] = self.src(k)[...]
+
+            self.hop(kind, k).start()
+
+        pl.when(self.below)(lambda: send(0, self.low, net.has_down))
+        pl.when(self.above)(lambda: send(1, self.high, net.has_up))
+
+    def finish(self, k):
+        net = self.net
+
+        @pl.when(self.middle)
+        def _():
+            self.hop(0, k).wait_recv()
+            total = self.src(k)[...].astype(F32) + self.low[k].astype(F32)
+            if self.two_sided:
+                self.hop(1, k).wait_recv()
+                total = total + self.high[k].astype(F32)
+            self.mine(k)[...] = total.astype(self.part.dtype)
+            self.hop(2, k).start()
+            if self.two_sided:
+                self.hop(3, k).start()
+
+        @pl.when(self.below)
+        def _():
+            self.hop(2, k).wait_recv()
+            pl.when(net.has_down)(lambda: self.hop(2, k).start())
+
+        @pl.when(self.above)
+        def _():
+            self.hop(3, k).wait_recv()
+            pl.when(net.has_up)(lambda: self.hop(3, k).start())
+
+        self.deliver(k)
+
+    def drain(self, k):
+        net = self.net
+        pl.when(self.below)(lambda: self.hop(0, k).wait_send())
+        pl.when(self.above)(lambda: self.hop(1, k).wait_send())
+        sends_down = jnp.logical_and(net.has_down, jnp.logical_not(self.above))
+        sends_up = jnp.logical_and(net.has_up, jnp.logical_not(self.below))
+        pl.when(sends_down)(lambda: self.hop(2, k).wait_send())
+        pl.when(sends_up)(lambda: self.hop(3, k).wait_send())
+
+
+def any_spec():
+    return pl.BlockSpec(memory_space=pl.ANY)
+
+
+def vmem_spec():
+    return pl.BlockSpec(memory_space=pltpu.VMEM)
+
+
+def params(cid, mib=60):
+    return pltpu.CompilerParams(
+        collective_id=cid, has_side_effects=True, vmem_limit_bytes=mib * 2**20
+    )
+
+
+def enter(tok, pos, gains, frequency, wq, wk, wv):
+    rows = tok.shape[0]
+    d_rows = wq.shape[0]
+    half = 4 * rows
+    n_sems = 48
+
+    def kernel(
+        tok_ref,
+        pos_ref,
+        gain_ref,
+        freq_ref,
+        wq_ref,
+        wk_ref,
+        wv_ref,
+        x_own,
+        n1,
+        raw_ref,
+        table,
+        core,
+        wall,
+        gains_ref,
+        wq_s,
+        wk_s,
+        wv_s,
+        wloc,
+        line,
+        toks,
+        pos_line,
+        poss,
+        heads,
+        gslots,
+        ssem,
+        rsem,
+        lsem,
+    ):
+        net = Net(ssem, rsem)
+        y, c = net.y, net.c
+        f = 2 * y + c
+        fy = 2 * (1 - y) + c
+        loads = [
+            pltpu.make_async_copy(a, b, lsem.at[k])
+            for k, (a, b) in enumerate(((wq_ref, wq_s), (wk_ref, wk_s), (wv_ref, wv_s)))
+        ]
+        for cp in loads:
+            cp.start()
+        net.greet()
+        pos_route = Route(net, pos_ref, pos_line, poss, 1)
+        route = Route(net, tok_ref, line, toks)
+        pos_route.start()
+        route.start()
+        g_core = net.new(gain_ref, gslots.at[f], net.to_core)
+        g_y = net.new(gain_ref, gslots.at[f], net.to_y)
+        g_relay = net.new(gslots.at[fy], gslots.at[fy], net.to_core)
+        g_core.start()
+        g_y.start()
+        gslots[f] = gain_ref[...]
+        for cp in loads:
+            cp.wait()
+        for t in range(4):
+            at = t * 4 * HD
+            wloc[t, :, 0 : 4 * HD] = wq_s[:, at : at + 4 * HD].astype(BF)
+            at = t * 2 * HD
+            wloc[t, :, 4 * HD : 6 * HD] = wk_s[:, at : at + 2 * HD].astype(BF)
+            wloc[t, :, 6 * HD : 8 * HD] = wv_s[:, at : at + 2 * HD].astype(BF)
+        w_y = net.new(wloc.at[net.sy], wall.at[f], net.to_y)
+        w_core = net.new(wloc.at[net.me], wall.at[f], net.to_core)
+        w_relay = net.new(wall.at[fy], wall.at[fy], net.to_core)
+        w_y.start()
+        w_core.start()
+        wall[f] = wloc[net.me]
+        pos_route.relay()
+        route.relay()
+        pos_route.enter()
+        route.enter()
+        pos_route.spread()
+        route.spread()
+        g_y.wait_recv()
+        g_relay.start()
+        w_y.wait_recv()
+        w_relay.start()
+        g_core.wait_recv()
+        g_relay.wait_recv()
+        w_core.wait_recv()
+        w_relay.wait_recv()
+        full = gslots[0] + gslots[1] + gslots[2] + gslots[3]
+        gains_ref[...] = full
+        attn_gain, q_gain, k_gain = full[0:1, :], full[2:3, 0:HD], full[3:4, 0:HD]
+        for j in range(2):
+            pos_route.wait(j)
+            route.wait(j)
+        x_own[...] = toks[net.me]
+        swaps = net.take(4)
+
+        def swap(k):
+            at = pl.ds(pl.multiple_of(k * rows, rows), rows)
+            return net.copy(swaps + k, heads.at[1 - c, at], core.at[c, at], net.to_core)
+
+        @pl.loop(0, 4)
+        def _(k):
+            at = pl.ds(pl.multiple_of(k * rows, rows), rows)
+            flat = toks[k].astype(F32)
+            normed = (flat * rms(flat) * attn_gain).astype(BF)
+            n1[at, :] = normed
+            raw = dot_nn(normed[:, 0:d_rows], wall[0])
+            for g in range(1, 4):
+                raw = raw + dot_nn(normed[:, g * d_rows : (g + 1) * d_rows], wall[g])
+            raw_ref[at, :] = raw[:, 0 : 6 * HD]
+            place = jnp.transpose(poss[k])
+            angles = jnp.concatenate(
+                [place[:, h : h + 1] * freq_ref[0:1, 0 : HD // 2] for h in range(rows // 128)],
+                axis=0,
+            )
+            cosine, sine = jnp.cos(angles), jnp.sin(angles)
+            table[at, :] = jnp.concatenate([cosine, sine], axis=-1)
+            cosine = jnp.concatenate([cosine, cosine], axis=-1)
+            sine = jnp.concatenate([-sine, sine], axis=-1)
+            for h in range(6):
+                u = raw[:, h * HD : (h + 1) * HD]
+                unit = u * rms(u) * (q_gain if h < 4 else k_gain)
+                turned = unit * cosine + pltpu.roll(unit, HD // 2, 1) * sine
+                g, lane = (h // 2, (h % 2) * HD) if h < 4 else (h - 4, 2 * HD)
+                heads[g, at, lane : lane + HD] = turned.astype(BF)
+            for g in range(2):
+                v = raw[:, (6 + g) * HD : (7 + g) * HD]
+                heads[g, at, 3 * HD : 4 * HD] = v.astype(BF)
+            swap(k).start()
+            core[c, at] = heads[c, at]
+
+        for k in range(4):
+            swap(k).wait()
+        for cp in (g_core, g_y, g_relay, w_core, w_y, w_relay):
+            cp.wait_send()
+        pos_route.drain()
+        route.drain()
+
+    vm = vmem_spec()
+    return pl.pallas_call(
+        kernel,
+        name="enter",
+        out_shape=[
+            shape((rows, D), BF),
+            shape((half, D), BF),
+            shape((half, 6 * HD), F32),
+            shape((half, HD), F32),
+            shape((2, half, 4 * HD), BF),
+            shape((4, d_rows, 8 * HD), BF),
+            shape((8, D), F32),
+        ],
+        in_specs=[vm] * 4 + [any_spec()] * 3,
+        out_specs=[vm] * 7,
+        scratch_shapes=[
+            pltpu.VMEM(wq.shape, F32),
+            pltpu.VMEM(wk.shape, F32),
+            pltpu.VMEM(wv.shape, F32),
+            pltpu.VMEM((4, d_rows, 8 * HD), BF),
+            pltpu.VMEM((4, rows, D), BF),
+            pltpu.VMEM((4, rows, D), BF),
+            pltpu.VMEM((4, 8, 128), F32),
+            pltpu.VMEM((4, 8, 128), F32),
+            pltpu.VMEM((2, half, 4 * HD), BF),
+            pltpu.VMEM((4, 8, D), F32),
+            pltpu.SemaphoreType.DMA((n_sems,)),
+            pltpu.SemaphoreType.DMA((n_sems,)),
+            pltpu.SemaphoreType.DMA((3,)),
+        ],
+        compiler_params=params(0),
+        cost_estimate=pl.CostEstimate(
+            flops=2 * half * D * 8 * HD, bytes_accessed=16 * 2**20, transcendentals=0
+        ),
+    )(tok, pos, gains, frequency, wq, wk, wv)
+
+
+def attend(block_map, inverse, core, cot, wg, wu, wo, wd):
+    half = core.shape[1]
+    length = 2 * half
+    tiles = length // QT
+    blocks = QT // BLK
+    n_blocks = length // BLK
+    factor = HD ** (-0.5) * LOG2E
+    rows = cot.shape[0]
+    d_rows = wg.shape[0]
+    unit = wg.shape[1] // 4
+    n_sems = 48
+
+    def kernel(
+        bm,
+        inv,
+        x_ref,
+        cot_ref,
+        wg_ref,
+        wu_ref,
+        wo_ref,
+        wd_ref,
+        att,
+        mixed,
+        lse_ref,
+        cots,
+        cot_own,
+        wgu,
+        wo_out,
+        wd_out,
+        q_s,
+        k_s,
+        v_s,
+        o_s,
+        wg_s,
+        wu_s,
+        wo_s,
+        wd_s,
+        wloc,
+        line,
+        ssem,
+        rsem,
+        lsem,
+    ):
+        net = Net(ssem, rsem)
+        x, y, c = net.x, net.y, net.c
+        f = 2 * y + c
+        fy = 2 * (1 - y) + c
+        loads = [
+            pltpu.make_async_copy(a, b, lsem.at[k])
+            for k, (a, b) in enumerate(
+                ((wg_ref, wg_s), (wu_ref, wu_s), (wo_ref, wo_s), (wd_ref, wd_s))
+            )
+        ]
+        for cp in loads:
+            cp.start()
+        net.greet()
+        route = Route(net, cot_ref, line, cots)
+        route.start()
+        w_y = net.new(wloc.at[net.sy], wgu.at[f], net.to_y)
+        w_core = net.new(wloc.at[net.me], wgu.at[f], net.to_core)
+        w_relay = net.new(wgu.at[fy], wgu.at[fy], net.to_core)
+        o_core = net.new(wo_out, wo_out, net.to_core)
+        d_core = net.new(wd_out, wd_out, net.to_core)
+        own = c == x
+
+        @pl.loop(0, tiles)
+        def _(i):
+            for h in range(blocks):
+                block = x_ref[inv[i * blocks + h]]
+                at = pl.multiple_of(i * QT, QT) + h * BLK
+                q_s[i, pl.ds(h * BLK, BLK), :] = block[:, 0:HD]
+                q_s[i, pl.ds(QT + h * BLK, BLK), :] = block[:, HD : 2 * HD]
+                k_s[pl.ds(at, BLK), :] = block[:, 2 * HD : 3 * HD]
+                v_s[pl.ds(at, BLK), 0:HD] = block[:, 3 * HD : 4 * HD]
+
+        v_s[:, HD : 2 * HD] = jnp.ones((length, HD), BF)
+        for cp in loads:
+            cp.wait()
+        for t in range(4):
+            wloc[t, :, 0:unit] = wg_s[:, t * unit : (t + 1) * unit].astype(BF)
+            wloc[t, :, unit : 2 * unit] = wu_s[:, t * unit : (t + 1) * unit].astype(BF)
+        w_y.start()
+        w_core.start()
+        wgu[f] = wloc[net.me]
+
+        @pl.when(own)
+        def _():
+            wo_out[...] = wo_s[...].astype(BF)
+            wd_out[...] = wd_s[...].astype(BF)
+            o_core.start()
+            d_core.start()
+
+        q_row = lax.broadcasted_iota(jnp.int32, (2 * QT, QT), 0)
+        k_row = lax.broadcasted_iota(jnp.int32, (2 * QT, QT), 1)
+        allowed = jnp.where(q_row >= QT, q_row - QT, q_row) >= k_row
+
+        def tile(i):
+            q = q_s[i]
+
+            def step(j, acc):
+                at = pl.ds(pl.multiple_of(j * QT, QT), QT)
+                p = jnp.exp2(dot_nt(q, k_s[at, :]) * factor).astype(BF)
+                return acc + dot_nn(p, v_s[at, :])
+
+            acc = lax.fori_loop(0, i, step, jnp.zeros((2 * QT, 2 * HD), F32))
+            at = pl.ds(pl.multiple_of(i * QT, QT), QT)
+            scores = jnp.where(allowed, dot_nt(q, k_s[at, :]) * factor, NEG)
+            acc = acc + dot_nn(jnp.exp2(scores).astype(BF), v_s[at, :])
+            total = acc[:, HD:]
+            out = acc[:, :HD] / total
+            lse_ref[i] = jnp.log2(jnp.transpose(total)[0:8, :])
+            for h in range(blocks):
+                for u in range(2):
+                    o_s[i * blocks + h, :, u * HD : (u + 1) * HD] = out[
+                        u * QT + h * BLK : u * QT + (h + 1) * BLK
+                    ].astype(BF)
+
+        @pl.loop(0, tiles)
+        def _(i):
+            tile(i)
+
+            @pl.when(i == tiles // 2)
+            def _():
+                route.relay()
+
+            @pl.when(i == tiles - 2)
+            def _():
+                route.enter()
+
+        route.spread()
+        w_y.wait_recv()
+        w_relay.start()
+        swap = net.take(1)
+
+        @pl.loop(0, n_blocks)
+        def _(s):
+            mixed[pl.ds(pl.multiple_of(s * BLK, BLK), BLK), :] = o_s[bm[s]]
+
+        away = mixed.at[pl.ds(pl.multiple_of((1 - c) * half, half), half)]
+        o_swap = net.copy(swap, away, att.at[c], net.to_core)
+        o_swap.start()
+        att[c] = mixed[pl.ds(pl.multiple_of(c * half, half), half), :]
+        pl.when(jnp.logical_not(own))(lambda: o_core.wait_recv())
+        pl.when(jnp.logical_not(own))(lambda: d_core.wait_recv())
+        w_core.wait_recv()
+        w_relay.wait_recv()
+        for j in range(2):
+            route.wait(j)
+        cot_own[...] = cots[net.me]
+        o_swap.wait()
+        pl.when(own)(lambda: o_core.wait_send())
+        pl.when(own)(lambda: d_core.wait_send())
+        for cp in (w_y, w_core, w_relay):
+            cp.wait_send()
+        route.drain()
+
+    vm = vmem_spec()
+    smem = pl.BlockSpec(memory_space=pltpu.SMEM)
+    return pl.pallas_call(
+        kernel,
+        name="attend",
+        out_shape=[
+            shape((2, half, 2 * HD), BF),
+            shape((length, 2 * HD), BF),
+            shape((tiles, 8, 2 * QT), F32),
+            shape((4, rows, D), BF),
+            shape((rows, D), BF),
+            shape((4, d_rows, 2 * unit), BF),
+            shape(wo.shape, BF),
+            shape(wd.shape, BF),
+        ],
+        in_specs=[smem, smem, vm, vm] + [any_spec()] * 4,
+        out_specs=[vm] * 8,
+        scratch_shapes=[
+            pltpu.VMEM((tiles, 2 * QT, HD), BF),
+            pltpu.VMEM((length, HD), BF),
+            pltpu.VMEM((length, 2 * HD), BF),
+            pltpu.VMEM((n_blocks, BLK, 2 * HD), BF),
+            pltpu.VMEM(wg.shape, F32),
+            pltpu.VMEM(wu.shape, F32),
+            pltpu.VMEM(wo.shape, F32),
+            pltpu.VMEM(wd.shape, F32),
+            pltpu.VMEM((4, d_rows, 2 * unit), BF),
+            pltpu.VMEM((4, rows, D), BF),
+            pltpu.SemaphoreType.DMA((n_sems,)),
+            pltpu.SemaphoreType.DMA((n_sems,)),
+            pltpu.SemaphoreType.DMA((4,)),
+        ],
+        compiler_params=params(1),
+        cost_estimate=pl.CostEstimate(
+            flops=2 * 2 * 2 * length * length * HD, bytes_accessed=16 * 2**20, transcendentals=0
+        ),
+    )(block_map, inverse, core.reshape(n_blocks, BLK, 4 * HD), cot, wg, wu, wo, wd)
+
+
+def feed_forward(att, x_own, wo, wgu, wd, cots, cot_own, gains):
+    half = att.shape[1]
+    rows = half // 4
+    unit = wd.shape[0]
+    d_rows = wgu.shape[1]
+    n_sems = 48
+
+    def kernel(
+        att_ref,
+        x_ref,
+        wo_ref,
+        wgu_ref,
+        wd_ref,
+        dy_ref,
+        cot_ref,
+        gain_ref,
+        core,
+        middle,
+        dmiddle,
+        result_part,
+        sum_gu,
+        sum_od,
+        mlp_gain_part,
+        part,
+        got,
+        mid,
+        n2,
+        hid,
+        dgu,
+        got2,
+        mid2,
+        dmb,
+        gm,
+        w_gu,
+        got_gu,
+        w_d,
+        got_d,
+        w_o,
+        got_o,
+        ssem,
+        rsem,
+    ):
+        net = Net(ssem, rsem)
+        c, me, sx, sy, sd = net.c, net.me, net.sx, net.sy, net.sd
+        mlp_gain = gain_ref[1:2, :]
+        net.greet(False)
+        out_sum = PlaneSum(net, part, got, mid)
+
+        def chunk(k):
+            return pl.ds(pl.multiple_of(k * rows, rows), rows)
+
+        def project(k):
+            part[k] = (
+                dot_nn(att_ref[0, chunk(k)], wo_ref[0 : 2 * HD, :])
+                + dot_nn(att_ref[1, chunk(k)], wo_ref[2 * HD : 4 * HD, :])
+            ).astype(BF)
+
+        project(sd)
+        out_sum.start_diagonal()
+        project(sx)
+        project(sy)
+        out_sum.start_sides()
+        project(me)
+        out_sum.forward()
+
+        def add_residual(at, total):
+            value = x_ref[at].astype(F32) + total
+            middle[at] = value
+            n2[me, at] = (value * rms(value) * mlp_gain).astype(BF)
+
+        out_sum.finish(add_residual)
+        gather = PlaneGather(net, n2.at[me], n2)
+        gather.start()
+
+        def forward_back(k):
+            rows_k = n2[k]
+            gate_up = dot_nn(rows_k[:, 0:d_rows], wgu_ref[0])
+            for g in range(1, 4):
+                gate_up = gate_up + dot_nn(rows_k[:, g * d_rows : (g + 1) * d_rows], wgu_ref[g])
+            gate, upward = gate_up[:, 0:unit], gate_up[:, unit : 2 * unit]
+            sigmoid = 1.0 / (1.0 + jnp.exp(-gate))
+            silu = gate * sigmoid
+            hid[k] = (silu * upward).astype(BF)
+            dh = dot_nt(dy_ref[k], wd_ref[...])
+            dgu[k, :, 0:unit] = (
+                dh * upward * sigmoid * (1.0 + gate * (1.0 - sigmoid))
+            ).astype(BF)
+            dgu[k, :, unit : 2 * unit] = (dh * silu).astype(BF)
+            grads = dgu[k]
+            for g in range(4):
+                part[k, :, g * d_rows : (g + 1) * d_rows] = dot_nt(grads, wgu_ref[g]).astype(BF)
+
+        out_sum.drain()
+        forward_back(me)
+        gather.forward()
+        gather.wait_sides()
+        back_sum = PlaneSum(net, part, got2, mid2)
+
+        @pl.loop(0, 2)
+        def _(n):
+            forward_back(jnp.where(n == 0, sx, sy))
+
+        back_sum.start_sides()
+        gather.wait_diagonal()
+        forward_back(sd)
+        back_sum.start_diagonal()
+
+        @pl.loop(0, 4)
+        def _(k):
+            result_part[k] = dot_nn(hid[k], wd_ref[...]).astype(BF)
+
+        back_sum.forward()
+        gu_sem = net.take(2)
+        d_sem = net.take(1)
+        o_sem = net.take(1)
+
+        def gu_copy(n):
+            return net.copy(gu_sem + n, w_gu.at[n], got_gu.at[n], net.to_core)
+
+        d_copy = net.copy(d_sem, w_d, got_d, net.to_core)
+        o_copy = net.copy(o_sem, w_o, got_o, net.to_core)
+        all_dgu = dgu.shape[2]
+
+        def slab(n, core_of):
+            f = 2 * n + core_of
+            at = pl.ds(pl.multiple_of(f * d_rows, d_rows), d_rows)
+            return dot_tn(n2[:, :, at].reshape(half, d_rows), dgu[...].reshape(half, all_dgu))
+
+        @pl.loop(0, 2)
+        def _(n):
+            w_gu[n] = slab(n, 1 - c).astype(BF)
+            gu_copy(n).start()
+
+        unit_half = unit // 2
+
+        def down(core_of):
+            at = pl.ds(pl.multiple_of(core_of * unit_half, unit_half), unit_half)
+            return dot_tn(hid[:, :, at].reshape(half, unit_half), dy_ref[...].reshape(half, D))
+
+        w_d[...] = down(1 - c).astype(BF)
+        d_copy.start()
+
+        def back_through_norm(at, dn2):
+            value = middle[at]
+            scale = rms(value)
+            w2 = dn2 * mlp_gain
+            grad = cot_ref[at].astype(F32) + norm_back(w2, value, scale)
+            dmiddle[at] = grad
+            dmb[me, at] = grad.astype(BF)
+            first = back_sum.half // 8
+            folded = jnp.sum((dn2 * value * scale).reshape(first, 8, D), axis=0)
+            mlp_gain_part[...] += folded
+
+        mlp_gain_part[...] = jnp.zeros_like(mlp_gain_part)
+        back_sum.finish(back_through_norm)
+        gather2 = PlaneGather(net, dmb.at[me], dmb)
+        gather2.start()
+        swap_sem = net.take(4)
+
+        def swap(k):
+            return net.copy(
+                swap_sem + k, gm.at[1 - c, chunk(k)], core.at[c, chunk(k)], net.to_core
+            )
+
+        def grad_mixed(k):
+            value = dot_nt(dmb[k], wo_ref[...]).astype(BF)
+            gm[0, chunk(k)] = value[:, 0 : 2 * HD]
+            gm[1, chunk(k)] = value[:, 2 * HD : 4 * HD]
+            swap(k).start()
+            core[c, chunk(k)] = gm[c, chunk(k)]
+
+        grad_mixed(me)
+
+        @pl.loop(0, 2)
+        def _(n):
+            value = slab(n, c)
+            gu_copy(n).wait_recv()
+            sum_gu[n] = (value + got_gu[n].astype(F32)).astype(BF)
+
+        gather2.forward()
+        value = down(c)
+        d_copy.wait_recv()
+        sum_od[0:unit_half] = (value + got_d[...].astype(F32)).astype(BF)
+        gather2.wait_sides()
+
+        @pl.loop(0, 2)
+        def _(n):
+            grad_mixed(jnp.where(n == 0, sx, sy))
+
+        gather2.wait_diagonal()
+        grad_mixed(sd)
+
+        def out_grad(g):
+            return dot_tn(att_ref[g], dmb[...].reshape(half, D))
+
+        w_o[...] = out_grad(1 - c).astype(BF)
+        o_copy.start()
+        value = out_grad(c)
+        o_copy.wait_recv()
+        sum_od[unit_half : unit_half + 2 * HD] = (value + got_o[...].astype(F32)).astype(BF)
+        for k in range(4):
+            swap(k).wait()
+        for n in range(2):
+            gu_copy(n).wait_send()
+        d_copy.wait_send()
+        o_copy.wait_send()
+        gather.drain()
+        gather2.drain()
+        back_sum.drain()
+
+    vm = vmem_spec()
+    half_rows = rows // 2
+    return pl.pallas_call(
+        kernel,
+        name="feed_forward",
+        out_shape=[
+            shape((2, half, 2 * HD), BF),
+            shape((rows, D), F32),
+            shape((rows, D), F32),
+            shape((4, rows, D), BF),
+            shape((2, d_rows, 2 * unit), BF),
+            shape((unit // 2 + 2 * HD, D), BF),
+            shape((8, D), F32),
+        ],
+        in_specs=[vm] * 8,
+        out_specs=[vm] * 7,
+        scratch_shapes=[
+            pltpu.VMEM((4, rows, D), BF),
+            pltpu.VMEM((6, half_rows, D), BF),
+            pltpu.VMEM((2, half_rows, D), BF),
+            pltpu.VMEM((4, rows, D), BF),
+            pltpu.VMEM((4, rows, unit), BF),
+            pltpu.VMEM((4, rows, 2 * unit), BF),
+            pltpu.VMEM((6, half_rows, D), BF),
+            pltpu.VMEM((2, half_rows, D), BF),
+            pltpu.VMEM((4, rows, D), BF),
+            pltpu.VMEM((2, half, 2 * HD), BF),
+            pltpu.VMEM((2, d_rows, 2 * unit), BF),
+            pltpu.VMEM((2, d_rows, 2 * unit), BF),
+            pltpu.VMEM((unit // 2, D), BF),
+            pltpu.VMEM((unit // 2, D), BF),
+            pltpu.VMEM((2 * HD, D), BF),
+            pltpu.VMEM((2 * HD, D), BF),
+            pltpu.SemaphoreType.DMA((n_sems,)),
+            pltpu.SemaphoreType.DMA((n_sems,)),
+        ],
+        compiler_params=params(2, 62),
+        cost_estimate=pl.CostEstimate(
+            flops=24 * half * D * unit, bytes_accessed=32 * 2**20, transcendentals=0
+        ),
+    )(att, x_own, wo, wgu, wd, cots, cot_own, gains)
+
+
+TILE = 64
+
+
+def attend_back(block_map, inverse, core, mixed, grad, lse, sum_od, sum_gu, result_part, middle):
+    half = core.shape[1]
+    length = 2 * half
+    tiles = length // QT
+    blocks = QT // BLK
+    n_blocks = length // BLK
+    scale = HD ** (-0.5)
+    factor = scale * LOG2E
+    rows = middle.shape[0]
+    od_tiles = sum_od.shape[0] // TILE
+    pairs = tiles * (tiles + 1) // 2
+    every = 3
+    n_sems = 4 * od_tiles + 3 * od_tiles + 16
+
+    def kernel(
+        bm,
+        inv,
+        x_ref,
+        o_ref,
+        g_ref,
+        lse_ref,
+        od_ref,
+        gu_ref,
+        rp_ref,
+        mid_ref,
+        dq,
+        result,
+        od_final,
+        gu_rows,
+        q_s,
+        g_s,
+        k_s,
+        v_s,
+        delta_s,
+        dq_s,
+        d_s,
+        d_c,
+        got,
+        mid,
+        low,
+        high,
+        part,
+        od_sum,
+        ssem,
+        rsem,
+    ):
+        net = Net(ssem, rsem)
+        x, y, c = net.x, net.y, net.c
+        net.greet(True, True)
+        total = PlaneSum(net, rp_ref, got, mid)
+        gu_y = net.new(gu_ref.at[1 - y], gu_rows.at[1], net.to_y)
+        swap = net.new(
+            d_s.at[pl.ds(pl.multiple_of((1 - c) * half, half), half)], dq.at[c], net.to_core
+        )
+        x_sem = net.take(2 * od_tiles)
+        chip_sem = net.take(od_tiles)
+        owner = device(net.z, 1 - x, y, x)
+        owns = c == x
+
+        def cross(k, h):
+            return net.copy(
+                x_sem + h * od_tiles + k, od_sum.at[k], od_final.at[h, k], owner
+            )
+
+        def chip(k, h):
+            return net.copy(chip_sem + k, od_sum.at[k], od_final.at[h, k], net.to_core)
+
+        def deliver(k):
+            cross(k, c).start()
+
+            @pl.when(owns)
+            def _():
+                od_final[c, k] = od_sum[k]
+
+            pl.when(jnp.logical_not(owns))(lambda: chip(k, c).start())
+
+        line = LineSum(
+            net,
+            od_tiles,
+            lambda k: od_ref.at[pl.ds(pl.multiple_of(k * TILE, TILE), TILE)],
+            lambda k: od_sum.at[k],
+            low,
+            high,
+            part,
+            deliver,
+        )
+        total.start_diagonal()
+        total.start_sides()
+        gu_y.start()
+        gu_rows[0] = gu_ref[y]
+        at_end = jnp.logical_or(net.z == 0, net.z == net.depth - 1)
+        lag = jnp.where(line.middle, 1, jnp.where(at_end, 6, 4))
+
+        @pl.when(at_end)
+        def _():
+            @pl.loop(0, od_tiles)
+            def _(k):
+                line.gather(k)
+
+        @pl.loop(0, tiles)
+        def _(i):
+            for h in range(blocks):
+                s = inv[i * blocks + h]
+                block, out, grad_ = x_ref[s], o_ref[s], g_ref[s]
+                at = pl.ds(pl.multiple_of(i * QT, QT) + h * BLK, BLK)
+                for u in range(2):
+                    to = pl.ds(u * QT + h * BLK, BLK)
+                    lanes = slice(u * HD, (u + 1) * HD)
+                    q_s[i, to, :] = block[:, lanes]
+                    g_s[i, to, :] = grad_[:, lanes]
+                    product = grad_[:, lanes].astype(F32) * out[:, lanes].astype(F32)
+                    delta_s[i, :, to] = jnp.broadcast_to(
+                        jnp.sum(jnp.transpose(product), axis=0, keepdims=True), (8, BLK)
+                    )
+                k_s[at, :] = block[:, 2 * HD : 3 * HD]
+                v_s[at, :] = block[:, 3 * HD : 4 * HD]
+
+        dq_s[...] = jnp.zeros_like(dq_s)
+        k_row = lax.broadcasted_iota(jnp.int32, (QT, 2 * QT), 0)
+        q_row = lax.broadcasted_iota(jnp.int32, (QT, 2 * QT), 1)
+        allowed = jnp.where(q_row >= QT, q_row - QT, q_row) >= k_row
+
+        def pump(n):
+            k = lax.div(n, every)
+            due = lax.rem(n, every) == 0
+
+            @pl.when(jnp.logical_and(due, jnp.logical_and(k < od_tiles, jnp.logical_not(at_end))))
+            def _():
+                line.gather(k)
+
+            @pl.when(jnp.logical_and(due, jnp.logical_and(k >= lag, k - lag < od_tiles)))
+            def _():
+                line.finish(k - lag)
+
+            pl.when(n == 10)(total.forward)
+
+        @pl.loop(0, tiles)
+        def _(j):
+            at = pl.ds(pl.multiple_of(j * QT, QT), QT)
+            k, v = k_s[at, :], v_s[at, :]
+            first = j * tiles - lax.div(j * (j - 1), 2)
+
+            def pair(i, carry, diagonal):
+                pump(first + i - j)
+                dk, dv = carry
+                q, g = q_s[i], g_s[i]
+                scores = dot_nt(k, q) * factor - lse_ref[i, 0:1, :]
+                if diagonal:
+                    scores = jnp.where(allowed, scores, NEG)
+                p = jnp.exp2(scores)
+                ds = (p * (dot_nt(v, g) - delta_s[i, 0:1, :])).astype(BF)
+                dq_s[i] += dot_tn(ds, k)
+                return (dk + dot_nn(ds, q), dv + dot_nn(p.astype(BF), g))
+
+            zero = jnp.zeros((QT, HD), F32)
+            carry = pair(j, (zero, zero), True)
+            dk, dv = lax.fori_loop(j + 1, tiles, lambda i, cr: pair(i, cr, False), carry)
+            for h in range(blocks):
+                part_ = slice(h * BLK, (h + 1) * BLK)
+                b = j * blocks + h
+                d_c[b, :, 2 * HD : 3 * HD] = (dk[part_] * scale).astype(BF)
+                d_c[b, :, 3 * HD : 4 * HD] = dv[part_].astype(BF)
+
+        @pl.loop(0, tiles)
+        def _(i):
+            for h in range(blocks):
+                for u in range(2):
+                    at = pl.ds(u * QT + h * BLK, BLK)
+                    d_c[i * blocks + h, :, u * HD : (u + 1) * HD] = (
+                        dq_s[i, at, :] * scale
+                    ).astype(BF)
+
+        @pl.loop(0, n_blocks)
+        def _(s):
+            d_s[pl.ds(pl.multiple_of(s * BLK, BLK), BLK), :] = d_c[bm[s]]
+
+        swap.start()
+        dq[c] = d_s[pl.ds(pl.multiple_of(c * half, half), half), :]
+
+        def add(at, value):
+            result[at] = (mid_ref[at] + value).astype(BF)
+
+        total.finish(add)
+        done_tiles = -(-pairs // every) - lag
+
+        @pl.loop(0, od_tiles)
+        def _(k):
+            pl.when(k >= done_tiles)(lambda: line.finish(k))
+
+        @pl.loop(0, od_tiles)
+        def _(k):
+            @pl.when(owns)
+            def _():
+                chip(k, 1 - c).wait_recv()
+
+            @pl.when(jnp.logical_not(owns))
+            def _():
+                for h in range(2):
+                    cross(k, h).wait_recv()
+                chip(k, c).wait_send()
+
+            cross(k, c).wait_send()
+            line.drain(k)
+
+        gu_y.wait()
+        swap.wait()
+        total.drain()
+
+    vm = vmem_spec()
+    smem = pl.BlockSpec(memory_space=pltpu.SMEM)
+    half_rows = rows // 2
+    slots = pltpu.VMEM((od_tiles, TILE, D), BF)
+    return pl.pallas_call(
+        kernel,
+        name="attend_back",
+        out_shape=[
+            shape((2, half, 4 * HD), BF),
+            shape((rows, D), BF),
+            shape((2, od_tiles, TILE, D), BF),
+            shape(sum_gu.shape, BF),
+        ],
+        in_specs=[smem, smem] + [vm] * 8,
+        out_specs=[vm] * 4,
+        scratch_shapes=[
+            pltpu.VMEM((tiles, 2 * QT, HD), BF),
+            pltpu.VMEM((tiles, 2 * QT, HD), BF),
+            pltpu.VMEM((length, HD), BF),
+            pltpu.VMEM((length, HD), BF),
+            pltpu.VMEM((tiles, 8, 2 * QT), F32),
+            pltpu.VMEM((tiles, 2 * QT, HD), F32),
+            pltpu.VMEM((length, 4 * HD), BF),
+            pltpu.VMEM((n_blocks, BLK, 4 * HD), BF),
+            pltpu.VMEM((6, half_rows, D), BF),
+            pltpu.VMEM((2, half_rows, D), BF),
+            slots,
+            slots,
+            slots,
+            slots,
+            pltpu.SemaphoreType.DMA((n_sems,)),
+            pltpu.SemaphoreType.DMA((n_sems,)),
+        ],
+        compiler_params=params(3),
+        cost_estimate=pl.CostEstimate(
+            flops=5 * 2 * 2 * length * length * HD, bytes_accessed=16 * 2**20, transcendentals=0
+        ),
+    )(
+        block_map,
+        inverse,
+        core.reshape(n_blocks, BLK, 4 * HD),
+        mixed.reshape(n_blocks, BLK, 2 * HD),
+        grad.reshape(n_blocks, BLK, 2 * HD),
+        lse,
+        sum_od,
+        sum_gu,
+        result_part,
+        middle,
+    )
+
+
+def leave(dq, raw, table, n1, wall, x_own, dmiddle, gains, result, gu_rows, mlp_gain_part):
+    half = n1.shape[0]
+    rows = half // 4
+    d_rows = wall.shape[1]
+    gu_cols = gu_rows.shape[2]
+    unit = gu_cols // 2
+    per = d_rows // TILE
+    tiles = 2 * per
+    n_sems = 2 * 5 * tiles + 40
+
+    def kernel(
+        dq_ref,
+        raw_ref,
+        table_ref,
+        n1_ref,
+        wall_ref,
+        x_ref,
+        dmid_ref,
+        gain_ref,
+        res_ref,
+        gu_ref,
+        mlp_ref,
+        result_out,
+        input_out,
+        out_q,
+        out_k,
+        out_v,
+        out_g,
+        out_u,
+        gain_out,
+        dcat,
+        part,
+        got,
+        mid,
+        grad_in,
+        w_out,
+        w_got,
+        w_sum,
+        w_rows,
+        gu_low,
+        gu_high,
+        gu_part,
+        gu_mine,
+        gu_other,
+        w_low,
+        w_high,
+        w_part,
+        w_mine,
+        w_other,
+        g_sum,
+        g_got,
+        g_low,
+        g_high,
+        g_part,
+        g_mine,
+        acc,
+        ssem,
+        rsem,
+    ):
+        net = Net(ssem, rsem)
+        z, x, y, c = net.z, net.x, net.y, net.c
+        stays = z == 2 * c + y
+        moves = jnp.logical_not(stays)
+        mate = device(2 * c + y, x, lax.rem(z, 2), lax.div(z, 2))
+        net.greet(True, False, (moves, mate))
+        res_copy = net.new(res_ref, result_out, mate)
+        in_copy = net.new(grad_in, input_out, mate)
+
+        def send_home(cp, src, dst):
+            pl.when(moves)(cp.start)
+
+            @pl.when(stays)
+            def _():
+                dst[...] = src[...]
+
+        def row_tile(ref):
+            def at(k):
+                return ref.at[lax.div(k, per), pl.ds(pl.multiple_of(lax.rem(k, per) * TILE, TILE), TILE)]
+
+            return at
+
+        gx_sem = net.take(tiles)
+        wx_sem = net.take(tiles)
+
+        def gu_cross(k):
+            return net.copy(gx_sem + k, gu_mine.at[k], gu_other.at[k], net.to_x)
+
+        def w_cross(k):
+            return net.copy(wx_sem + k, w_mine.at[k], w_other.at[k], net.to_x)
+
+        gu_line = LineSum(
+            net,
+            tiles,
+            row_tile(gu_ref),
+            lambda k: gu_mine.at[k],
+            gu_low,
+            gu_high,
+            gu_part,
+            lambda k: gu_cross(k).start(),
+        )
+        w_line = LineSum(
+            net,
+            tiles,
+            row_tile(w_rows),
+            lambda k: w_mine.at[k],
+            w_low,
+            w_high,
+            w_part,
+            lambda k: w_cross(k).start(),
+        )
+        g_line = LineSum(
+            net,
+            1,
+            lambda k: g_sum.at[0],
+            lambda k: g_mine.at[0],
+            g_low,
+            g_high,
+            g_part,
+            lambda k: None,
+        )
+        at_end = jnp.logical_or(z == 0, z == net.depth - 1)
+
+        @pl.when(at_end)
+        def _():
+            @pl.loop(0, tiles)
+            def _(k):
+                gu_line.gather(k)
+
+        def gu_gather(k):
+            pl.when(jnp.logical_not(at_end))(lambda: gu_line.gather(k))
+
+        send_home(res_copy, res_ref, result_out)
+        total = PlaneSum(net, part, got, mid)
+        attn_gain, q_gain, k_gain = gain_ref[0:1, :], gain_ref[2:3, 0:HD], gain_ref[3:4, 0:HD]
+        acc[...] = jnp.zeros_like(acc)
+
+        def fold(v):
+            return jnp.sum(v.reshape(v.shape[0] // 8, 8, v.shape[1]), axis=0)
+
+        def chunk(k):
+            at = pl.ds(pl.multiple_of(k * rows, rows), rows)
+            half_w = HD // 2
+            cosine, sine = table_ref[at, 0:half_w], table_ref[at, half_w:HD]
+            cosine = jnp.concatenate([cosine, cosine], axis=-1)
+            sine = jnp.concatenate([-sine, sine], axis=-1)
+            for h in range(6):
+                g, lane = (h // 2, (h % 2) * HD) if h < 4 else (h - 4, 2 * HD)
+                gain = q_gain if h < 4 else k_gain
+                grad = dq_ref[g, at, lane : lane + HD].astype(F32)
+                du = grad * cosine - pltpu.roll(grad, half_w, 1) * sine
+                u = raw_ref[at, h * HD : (h + 1) * HD]
+                scale = rms(u)
+                lanes = slice(0, HD) if h < 4 else slice(HD, 2 * HD)
+                acc[2, :, lanes] += fold(du * u * scale)
+                dcat[at, h * HD : (h + 1) * HD] = norm_back(du * gain, u, scale).astype(BF)
+            for g in range(2):
+                dcat[at, (6 + g) * HD : (7 + g) * HD] = dq_ref[g, at, 3 * HD : 4 * HD]
+            d = dcat[at, :]
+            for g in range(4):
+                part[k, :, g * d_rows : (g + 1) * d_rows] = dot_nt(d, wall_ref[g]).astype(BF)
+
+        chunk(net.sd)
+        total.start_diagonal()
+        gu_gather(0)
+
+        @pl.loop(0, 2)
+        def _(n):
+            chunk(jnp.where(n == 0, net.sx, net.sy))
+
+        total.start_sides()
+        gu_gather(1)
+        chunk(net.me)
+        pl.when(gu_line.middle)(lambda: gu_line.finish(0))
+        gu_gather(2)
+        total.forward()
+
+        def slab(n, core_of):
+            f = 2 * n + core_of
+            at = pl.ds(pl.multiple_of(f * d_rows, d_rows), d_rows)
+            return dot_tn(n1_ref[:, at], dcat[...])
+
+        w_sem = net.take(2)
+
+        def w_copy(n):
+            return net.copy(w_sem + n, w_out.at[n], w_got.at[n], net.to_core)
+
+        @pl.loop(0, 2)
+        def _(n):
+            w_out[n] = slab(n, 1 - c).astype(BF)
+            w_copy(n).start()
+
+        pl.when(gu_line.middle)(lambda: gu_line.finish(1))
+        gu_gather(3)
+
+        w_y = net.new(w_sum, w_rows.at[1], net.to_y)
+        value = slab(1 - y, c)
+        w_copy(1 - y).wait_recv()
+        w_sum[...] = (value + w_got[1 - y].astype(F32)).astype(BF)
+        w_y.start()
+        value = slab(y, c)
+        w_copy(y).wait_recv()
+        w_rows[0] = (value + w_got[y].astype(F32)).astype(BF)
+        pl.when(gu_line.middle)(lambda: gu_line.finish(2))
+        gu_gather(4)
+
+        def back_through_norm(at, dn1):
+            value = x_ref[at].astype(F32)
+            scale = rms(value)
+            acc[0] += fold(dn1 * value * scale)
+            grad_in[at] = (dmid_ref[at] + norm_back(dn1 * attn_gain, value, scale)).astype(BF)
+
+        total.finish(back_through_norm)
+        send_home(in_copy, grad_in, input_out)
+        acc[1] = mlp_ref[...]
+        for row in range(3):
+            g_sum[0, row : row + 1, :] = jnp.sum(acc[row], axis=0, keepdims=True)
+        g_sum[0, 3:8, :] = jnp.zeros((5, D), F32)
+        g_swaps = []
+        for n, to in enumerate((net.to_core, net.to_y, net.to_x)):
+            cp = net.new(g_sum.at[0], g_got.at[n], to)
+            cp.start()
+            pl.when(gu_line.middle)(lambda: gu_line.finish(3 + n))
+            gu_gather(5 + n) if 5 + n < tiles else None
+            cp.wait()
+            g_sum[0] = g_sum[0] + g_got[n]
+        g_line.gather(0)
+
+        @pl.when(at_end)
+        def _():
+            @pl.loop(0, per)
+            def _(k):
+                w_line.gather(k)
+
+            w_y.wait_recv()
+
+            @pl.loop(per, tiles)
+            def _(k):
+                w_line.gather(k)
+
+            @pl.loop(0, tiles)
+            def _(k):
+                gu_line.finish(k)
+
+            g_line.finish(0)
+
+            @pl.loop(0, tiles)
+            def _(k):
+                w_line.finish(k)
+
+        @pl.when(line_between(net, gu_line, at_end))
+        def _():
+            @pl.loop(0, tiles)
+            def _(k):
+                gu_line.finish(k)
+                pl.when(k == per)(w_y.wait_recv)
+                w_line.gather(k)
+
+            g_line.finish(0)
+
+            @pl.loop(0, tiles)
+            def _(k):
+                w_line.finish(k)
+
+        @pl.when(gu_line.middle)
+        def _():
+            @pl.loop(6, tiles)
+            def _(k):
+                gu_line.finish(k)
+
+            g_line.finish(0)
+
+            @pl.loop(0, tiles)
+            def _(k):
+                pl.when(k == per)(w_y.wait_recv)
+                w_line.finish(k)
+
+        gain_out[...] = g_mine[0]
+
+        def place(mine, copies, outs, widths):
+            @pl.loop(0, tiles)
+            def _(k):
+                copies(k).wait_recv()
+                row_half = jnp.where(k < per, y, 1 - y)
+                at = pl.ds(pl.multiple_of(lax.rem(k, per) * TILE, TILE), TILE)
+                for slots, x_of in ((mine[0], x), (mine[1], 1 - x)):
+                    quarter = 2 * row_half + x_of
+                    first = 0
+                    for out, width in zip(outs, widths):
+                        lanes = pl.ds(pl.multiple_of(quarter * width, width), width)
+                        out[at, lanes] = slots[k, :, first : first + width]
+                        first += width
+
+        place((gu_mine, gu_other), gu_cross, (out_g, out_u), (unit, unit))
+        place((w_mine, w_other), w_cross, (out_q, out_k, out_v), (4 * HD, 2 * HD, 2 * HD))
+
+        @pl.loop(0, tiles)
+        def _(k):
+            gu_line.drain(k)
+            w_line.drain(k)
+            gu_cross(k).wait_send()
+            w_cross(k).wait_send()
+
+        g_line.drain(0)
+        for n in range(2):
+            w_copy(n).wait_send()
+        w_y.wait_send()
+        total.drain()
+        pl.when(moves)(lambda: res_copy.wait())
+        pl.when(moves)(lambda: in_copy.wait())
+
+    def line_between(net, line, at_end):
+        return jnp.logical_not(jnp.logical_or(line.middle, at_end))
+
+    vm = vmem_spec()
+    half_rows = rows // 2
+    gu_slots = pltpu.VMEM((tiles, TILE, gu_cols), BF)
+    w_slots = pltpu.VMEM((tiles, TILE, 8 * HD), BF)
+    g_slot = pltpu.VMEM((1, 8, D), F32)
+    return pl.pallas_call(
+        kernel,
+        name="leave",
+        out_shape=[
+            shape((rows, D), BF),
+            shape((rows, D), BF),
+            shape((d_rows, 16 * HD), BF),
+            shape((d_rows, 8 * HD), BF),
+            shape((d_rows, 8 * HD), BF),
+            shape((d_rows, 4 * unit), BF),
+            shape((d_rows, 4 * unit), BF),
+            shape((8, D), F32),
+        ],
+        in_specs=[vm] * 11,
+        out_specs=[vm] * 8,
+        scratch_shapes=[
+            pltpu.VMEM((half, 8 * HD), BF),
+            pltpu.VMEM((4, rows, D), BF),
+            pltpu.VMEM((6, half_rows, D), BF),
+            pltpu.VMEM((2, half_rows, D), BF),
+            pltpu.VMEM((rows, D), BF),
+            pltpu.VMEM((2, d_rows, 8 * HD), BF),
+            pltpu.VMEM((2, d_rows, 8 * HD), BF),
+            pltpu.VMEM((d_rows, 8 * HD), BF),
+            pltpu.VMEM((2, d_rows, 8 * HD), BF),
+        ]
+        + [gu_slots] * 5
+        + [w_slots] * 5
+        + [g_slot, pltpu.VMEM((3, 8, D), F32)]
+        + [g_slot] * 4
+        + [
+            pltpu.VMEM((3, 8, D), F32),
+            pltpu.SemaphoreType.DMA((n_sems,)),
+            pltpu.SemaphoreType.DMA((n_sems,)),
+        ],
+        compiler_params=params(4, 62),
+        cost_estimate=pl.CostEstimate(
+            flops=4 * half * D * 8 * HD, bytes_accessed=32 * 2**20, transcendentals=0
+        ),
+    )(dq, raw, table, n1, wall, x_own, dmiddle, gains, result, gu_rows, mlp_gain_part)
+
+
+def plane_body(
+    tokens,
+    cotangent,
+    block_map,
+    positions,
+    attn_gain,
+    query_weight,
+    key_weight,
+    value_weight,
+    query_gain,
+    key_gain,
+    out_weight,
+    mlp_gain,
+    gate_weight,
+    up_weight,
+    down_weight,
+):
+    z, x, y, c = coords()
+    f = 2 * y + c
+    rows = tokens.shape[1]
+    parts = lax.axis_size("fsdp")
+
+    def spread_out(gain):
+        n = gain.shape[0]
+        full = jnp.concatenate([gain] * parts)
+        kept = jnp.where(jnp.arange(n * parts) // n == f, full, 0.0)
+        return jnp.pad(kept, (0, D - n * parts))
+
+    gains = jnp.stack(
+        [spread_out(g) for g in (attn_gain, mlp_gain, query_gain, key_gain)]
+        + [jnp.zeros((D,), F32)] * 4
+    )
+    pos = jnp.pad(positions.reshape(rows // 128, 128).astype(F32), ((0, 8 - rows // 128), (0, 0)))
+    frequency = jnp.exp(
+        jnp.arange(0, HD, 2).astype(F32) * (-math.log(theta_base) / HD)
+    )
+    frequency = jnp.broadcast_to(jnp.pad(frequency, (0, HD // 2))[None], (8, HD))
+    flat_map = block_map.reshape(-1)
+    n_blocks = flat_map.shape[0]
+    order = jnp.arange(n_blocks, dtype=jnp.int32)
+    inverse = jnp.sum(
+        jnp.where(flat_map[None, :] == order[:, None], order[None, :], 0), axis=1
+    ).astype(jnp.int32)
+    x_own, n1, raw, table, core, wall, gains = enter(
+        tokens.reshape(rows, D),
+        pos,
+        gains,
+        frequency,
+        query_weight,
+        key_weight,
+        value_weight,
+    )
+    att, mixed, lse, cots, cot_own, wgu, wo, wd = attend(
+        flat_map,
+        inverse,
+        core,
+        cotangent.reshape(rows, D),
+        gate_weight,
+        up_weight,
+        out_weight,
+        down_weight,
+    )
+    grad, middle, dmiddle, result_part, sum_gu, sum_od, mlp_gain_part = feed_forward(
+        att, x_own, wo, wgu, wd, cots, cot_own, gains
+    )
+    dq, result, od, gu_rows = attend_back(
+        flat_map, inverse, core, mixed, grad, lse, sum_od, sum_gu, result_part, middle
+    )
+    result, input_grad, grad_q, grad_k, grad_v, grad_g, grad_u, gain_sums = leave(
+        dq, raw, table, n1, wall, x_own, dmiddle, gains, result, gu_rows, mlp_gain_part
+    )
+    od = od.reshape(2, -1, D)
+    down_half = down_weight.shape[0] // 2
+
+    def own_gain(values, size):
+        return lax.dynamic_slice_in_dim(values, f * (size // parts), size // parts)
+
+    return (
+        result.astype(F32).reshape(tokens.shape),
+        input_grad.astype(F32).reshape(tokens.shape),
+        own_gain(gain_sums[0], D),
+        grad_q.astype(F32),
+        grad_k.astype(F32),
+        grad_v.astype(F32),
+        own_gain(gain_sums[2, :HD], HD),
+        own_gain(gain_sums[2, HD : 2 * HD], HD),
+        od[:, down_half:].reshape(out_weight.shape).astype(F32),
+        own_gain(gain_sums[1], D),
+        grad_g.astype(F32),
+        grad_u.astype(F32),
+        od[:, :down_half].reshape(down_weight.shape).astype(F32),
+    )
+
+
 def solution(mesh):
     placed = (
         P("fsdp", "ctx", None),
@@ -339,8 +2096,9 @@
         P("fsdp", None),
         P("fsdp", None),
     )
+    fits = mesh.shape["fsdp"] == 4 and mesh.shape["ctx"] == 8
     return jax.shard_map(
-        body,
+        plane_body if fits else body,
         mesh=mesh,
         in_specs=placed,
         out_specs=(

time: 1400 us -> 432 us (0.31)
  waiting for transfers between devices: 981 us -> 0 us
  Pallas kernels: 0 us -> 399 us
  matrix products: 216 us -> 0 us
  local copies, waits for them, and re-layouts: 70.1 us -> 6.07 us
  blocking collectives: 46 us -> 0 us
  other arithmetic: 63.2 us -> 18.3 us
  between operations: 17 us -> 1.2 us
    reduce_scatter x9 -> x0, waiting for transfers between devices: 483 us -> none  [the longest x1 87.4 us: body(): lax.psum_scatter(grad_values_all.astype(jnp.bfloat16), 'ctx', scatter_dim...]
    pallas_call x0 -> x5, Pallas kernels: none -> 399 us  [the longest x1 130 us: leave(): pl.pallas_call(kernel, name='leave', out_shape=[shape((rows, D), BF), sha...]
    all_gather x9 -> x0, waiting for transfers between devices: 278 us -> none  [the longest x1 63.1 us: body(): keys_all = lax.all_gather(key_seq[seq_item], 'ctx', axis=0, tiled=True)]
    psum x1 -> x0, waiting for transfers between devices: 219 us -> none  [body(): lax.psum(shares[1].astype(jnp.bfloat16), 'ctx').astype(jnp.float32)]
    dot_general x77 -> x0, matrix products: 216 us -> none  [the longest x16 33.8 us: score_block(): jnp.einsum('qgd,sd->gqs', grouped, keys_head, preferred_element_type=jnp....]
    unnamed x105 -> x19, local copies, waits for them, and re-layouts: 29.3 us -> 0.12 us
    convert_element_type x32 -> x8, other arithmetic: 40.7 us -> 13.8 us  [the longest x1 3.55 us: plane_body(): grad_g.astype(F32)]
    psum x1 -> x0, blocking collectives: 22.5 us -> none  [body(): lax.psum(shares[0].astype(jnp.bfloat16), 'ctx').astype(jnp.float32)]
  transfers between devices with their start and end apart: 19 -> 0, of which waited for: 18 -> 0; matrix products, arithmetic and copies ran while one was open for 12% -> 0% of each run, Pallas kernels for 0% -> 0%
where the time goes in v2:
time: 432 us; the launch traced here: 424 us
  Pallas kernels  399 us (92%)
  other arithmetic  18.3 us (4%)
  local copies, waits for them, and re-layouts  6.07 us (1%)
    pallas_call x1, Pallas kernels, leave(): pl.pallas_call(kernel, name='leave', out_shape=[shape((rows, D), BF), sha...  130 us
    pallas_call x1, Pallas kernels, feed_forward(): pl.pallas_call(kernel, name='feed_forward', out_shape=[shape((2, half, 2...  94.4 us
    pallas_call x1, Pallas kernels, attend_back(): pl.pallas_call(kernel, name='attend_back', out_shape=[shape((2, half, 4 *...  62.5 us
    pallas_call x1, Pallas kernels, enter(): pl.pallas_call(kernel, name='enter', out_shape=[shape((rows, D), BF), sha...  56.2 us
    pallas_call x1, Pallas kernels, attend(): pl.pallas_call(kernel, name='attend', out_shape=[shape((2, half, 2 * HD),...  55.7 us

profile of v2, /device:TPU:0, one launch (start us, length us, event | category | flops | bytes accessed | tf_op | source)
XLA Modules:
  0.0 424.2 jit_solution(4853893311609317276)
XLA Ops:
  0.6 0.8 compare_select_fusion
  1.5 0.9 compare_select_fusion.2
  2.4 0.7 stack.17.gain_ref
  3.1 0.6 broadcast_in_dim.34.freq_ref
  3.7 0.7 convert_element_type.45
  4.4 0.6 pad.15.pos_ref
  5.0 0.0 copy-start.7
  5.0 56.2 %enter.1 = (bf16[256,1024]{1,0:T(8,128)(2,1)}, bf16[1024,1024]{1,0:T(8,128)(2,1)}, f32[1024,768]{1,0:T(8,128)}, f32[1024,128]{1,0:T(8,128)}, bf16[2,1024,512]{2,...) custom-call(bf16[256,1024]{1,0:T(8,128)(2,1)} %bitcast.38, f32[8,128]{1,0:T(8,128)} %pad.15.pos_ref, ...), custom_call_target="tpu_custom_call" | custom-call | flops 2147483648 | bytes 16777216 | tf_op jit(solution)/shard_map/enter/pallas_call | solution.py:881
  61.1 0.0 copy-done.7
  61.2 0.1 copy.30
  61.2 0.1 reshape.222.bm
  61.3 0.0 copy-start.8
  61.3 0.6 select_reduce_fusion.inv
  62.0 0.0 copy-done.8
  62.0 55.7 %attend.1 = (bf16[2,1024,256]{2,1,0:T(8,128)(2,1)}, bf16[2048,256]{1,0:T(8,128)(2,1)}, f32[8,8,512]{2,1,0:T(8,128)}, bf16[4,256,1024]{2,1,0:T(8,128)(2,1)}, bf16...) custom-call(s32[16]{0:T(128)} %copy-done.8, ...), custom_call_target="tpu_custom_call" | custom-call | flops 4294967296 | bytes 16777216 | tf_op jit(solution)/shard_map/attend/pallas_call | solution.py:1075
  117.7 94.4 %feed_forward.1 = (bf16[2,1024,256]{2,1,0:T(8,128)(2,1)}, f32[256,1024]{1,0:T(8,128)}, f32[256,1024]{1,0:T(8,128)}, bf16[4,256,1024]{2,1,0:T(8,128)(2,1)}, bf16[...) custom-call(bf16[2,1024,256]{2,1,0:T(8,128)(2,1)} %get-tuple-element.49.att_ref, ...), custom_call_target="tpu_custom_call" | custom-call | flops 19327352832 | bytes 33554432 | tf_op jit(solution)/shard_map/feed_forward/pallas_call | solution.py:1324
  212.0 62.5 %attend_back.1 = (bf16[2,1024,512]{2,1,0:T(8,128)(2,1)}, bf16[256,1024]{1,0:T(8,128)(2,1)}, bf16[2,10,64,1024]{3,2,1,0:T(8,128)(2,1)}, bf16[2,256,1536]{2,1,0:T(8,128)(2,1)}) custom-call(s32[16]{0:T(128)} %copy-done.8, s32[16]{0:T(128)} %select_reduce_fusion.inv, bf16[16,128,512]{2,1,0:T(8,128)(2,1)} %bitcast.41, bf16[16,128,256]{2,1,0:T(8,128)(2,1)} %bitcast.42, ...), custom_call_target="tpu_custom_call" | custom-call | flops 10737418240 | bytes 16777216 | tf_op jit(solution)/shard_map/attend_back/pallas_call | solution.py:1580
  274.5 129.9 %leave.1 = (bf16[256,1024]{1,0:T(8,128)(2,1)}, bf16[256,1024]{1,0:T(8,128)(2,1)}, bf16[256,2048]{1,0:T(8,128)(2,1)}, bf16[256,1024]{1,0:T(8,128)(2,1)}, bf16[256...) custom-call(bf16[2,1024,512]{2,1,0:T(8,128)(2,1)} %get-tuple-element.63.dq_ref, ...), custom_call_target="tpu_custom_call" | custom-call | flops 4294967296 | bytes 33554432 | tf_op jit(solution)/shard_map/leave/pallas_call | solution.py:1945
  404.4 0.0 copy-start.1
  404.4 3.6 convert_element_type.53
  408.0 0.0 copy-done.1
  408.0 0.0 copy-start.2
  408.0 2.0 convert_element_type.54
  410.0 0.0 copy-start.6
  410.0 0.0 copy-done.2
  410.0 0.0 copy-start.5
  410.0 1.6 convert_element_type.48
  411.6 0.0 copy-start.4
  411.6 0.0 copy-done.6
  411.6 0.0 copy-start.3
  411.6 1.1 bitcast_convert_fusion.2
  412.6 0.0 copy-done.5
  412.6 0.0 copy-start
  412.7 1.1 bitcast_convert_fusion.3
  413.7 0.0 copy-done.4
  413.7 1.1 convert_element_type.49
  414.8 0.0 copy-done.3
  414.8 1.1 convert_element_type.50
  415.9 0.8 fusion.2
  416.8 0.6 constant_dynamic-slice_fusion.2
  417.3 0.6 constant_dynamic-slice_fusion.3
  417.9 0.7 fusion.3
  418.6 0.6 fusion
  419.2 0.6 fusion.1
  419.7 0.0 copy-done
  419.7 0.1 slice.25
  419.9 2.2 bitcast_convert_fusion
  422.0 0.1 slice.24
  422.1 1.6 bitcast_convert_fusion.1
  (5 shorter events, 0.0 us)
Async XLA Ops:
  5.0 56.2 %copy-start.7 = (s32[8,2]{0,1:T(2,128)S(1)}, s32[8,2]{0,1:T(2,128)}, u32[]{:S(2)}) copy-start(s32[8,2]{0,1:T(2,128)} %param.17) | copy-start | bytes 196
  61.3 0.6 copy-start.8
  404.4 3.6 copy-start.1
  408.0 2.0 copy-start.2
  410.0 1.6 copy-start.6
  410.0 2.7 copy-start.5
  411.6 2.2 copy-start.4
  411.6 3.3 copy-start.3
  412.6 7.1 %copy-start = (bf16[2,10,64,1024]{3,2,1,0:T(8,128)(2,1)S(1)}, bf16[2,10,64,1024]{3,2,1,0:T(8,128)(2,1)}, u32[]{:S(2)}) copy-start(bf16[2,10,64,1024]{3,2,1,0:T(8,128)(2,1)} %get-tuple-element.78) | copy-start | bytes 7864324
